TPU v7x, 32 devices: a whole 2x2x4 slice. The times are simulated.
32 devices in a mesh: groups: 1, cache: 16 (over z, y, x), dp: 2 (over core).
Axes of the slice: x: 2, y: 2, z: 4, core: 2. Of those that a mesh axis runs over, the one named last changes fastest.
Arguments:
- hidden: bfloat16 [640, 8192], P(('groups', 'dp'), 'cache'), may hold values from -6 to 6
- out_grad: bfloat16 [640, 8192], P(('groups', 'dp'), 'cache'), may hold values from -192 to 192
- norm_gain: float32 [8192], replicated, may hold values from 0.25 to 1.75
- w_query: bfloat16 [8192, 2048], P(None, 'cache'), may hold values from -0.0625 to 0.0625
- w_key: bfloat16 [8192, 8, 128], P(None, None, 'cache'), may hold values from -0.1875 to 0.1875
- w_value: bfloat16 [8192, 8, 128], P(None, None, 'cache'), may hold values from -0.0625 to 0.0625
- w_out: bfloat16 [2048, 8192], P('cache'), may hold values from -0.125 to 0.125
- cache_keys: float32 [1024, 1024], P(('groups', 'cache', 'dp')), may hold values from -512 to 512
- cache_values: float32 [1024, 1024], P(('groups', 'cache', 'dp')), may hold values from -6 to 6
- first_moment: float32 [2, 1024, 1024], P(None, ('groups', 'cache', 'dp')), may hold values from -0.1875 to 0.1875
- second_moment: float32 [2, 1024, 1024], P(None, ('groups', 'cache', 'dp')), may hold values from 0.0001 to 0.002
- conv_lengths: int32 [2, 4], P(('groups', 'dp')), may hold values from 1 to 160, 320 in all within a row
- row_offsets: int32 [2, 4], P(('groups', 'dp')), may hold values from 0 to 1023
Outputs:
- new_keys: float32 [1024, 1024], P(('groups', 'cache', 'dp'))
- new_values: float32 [1024, 1024], P(('groups', 'cache', 'dp'))
- new_first: float32 [2, 1024, 1024], P(None, ('groups', 'cache', 'dp'))
- new_second: float32 [2, 1024, 1024], P(None, ('groups', 'cache', 'dp'))
Inputs may be any that keep to these rules, and one draw needn't show every extreme that they name: `conv_lengths`: each dp index's 4 lengths sum to 320, and one of them is 160.
All inputs are finite; a program needn't handle non-finite values.
Results may differ from a plain program's by a relative error of at most 0.006.
The roundings to bfloat16 on the way count: a program that leaves them out, or rounds other values in their place, can miss the bound.
Values may be sent and summed in bfloat16 or wider, within the bound.
A program may use at most 128 MiB of HBM per device.

v0:
```python
import math

import jax
import jax.numpy as jnp
from jax import lax
from jax.sharding import PartitionSpec as P

KV = 8
ADAM_STEP = 10


THETA = 500000.0
BETA_ONE = 0.9
BETA_TWO = 0.999
RATE = 0.02
EPSILON = 1e-08


def rope_tables(position, head_width):
    half_width = head_width // 2
    inverse = jnp.exp(
        jnp.arange(half_width, dtype=jnp.float32) * (-2.0 * math.log(THETA) / head_width)
    )
    angles = position.astype(jnp.float32)[:, None] * inverse[None, :]
    return (jnp.cos(angles), jnp.sin(angles))


def rotate(tensor, cos_table, sin_table):
    half_width = tensor.shape[1] // 2
    first_half = tensor[:, :half_width]
    second_half = tensor[:, half_width:]
    return jnp.concatenate(
        [
            first_half * cos_table - second_half * sin_table,
            second_half * cos_table + first_half * sin_table,
        ],
        axis=1,
    )


def row_layout(lengths, offsets, row_count, cache_len):
    end_rows = jnp.cumsum(lengths)
    start_rows = end_rows - lengths
    row_index = jnp.arange(row_count, dtype=jnp.int32)
    segment = jnp.sum((row_index[:, None] >= end_rows[None, :]).astype(jnp.int32), axis=1)
    onehot = segment[:, None] == jnp.arange(lengths.shape[0], dtype=jnp.int32)[None, :]
    first_row = jnp.sum(jnp.where(onehot, start_rows[None, :], 0), axis=1)
    offset_row = jnp.sum(jnp.where(onehot, offsets[None, :], 0), axis=1)
    return (segment, cache_len + offset_row + row_index - first_row)


def attend(query, grad_out, cache_k, cache_v, self_k, self_v, allowed, score_scale):
    contract = (((1,), (1,)), ((), ()))
    score_cache = (
        lax.dot_general(query, cache_k, contract, preferred_element_type=jnp.float32) * score_scale
    )
    score_self = (
        lax.dot_general(query, self_k, contract, preferred_element_type=jnp.float32) * score_scale
    )
    score_self = jnp.where(allowed, score_self, -1e30)
    highest = jnp.maximum(
        jnp.max(score_cache, axis=1, keepdims=True), jnp.max(score_self, axis=1, keepdims=True)
    )
    exp_cache = jnp.exp(score_cache - highest)
    exp_self = jnp.exp(score_self - highest)
    denominator = jnp.sum(exp_cache, axis=1, keepdims=True) + jnp.sum(
        exp_self, axis=1, keepdims=True
    )
    prob_cache = exp_cache / denominator
    prob_self = exp_self / denominator
    weight_cache = prob_cache.astype(jnp.bfloat16)
    weight_self = prob_self.astype(jnp.bfloat16)
    attended = jnp.dot(weight_cache, cache_v, preferred_element_type=jnp.float32) + jnp.dot(
        weight_self, self_v, preferred_element_type=jnp.float32
    )
    delta_row = jnp.sum(grad_out.astype(jnp.float32) * attended, axis=1, keepdims=True)
    grad_prob = lax.dot_general(grad_out, cache_v, contract, preferred_element_type=jnp.float32)
    grad_score = (prob_cache * (grad_prob - delta_row)).astype(jnp.bfloat16)
    return (grad_score, weight_cache)


def adam_update(master, gradient, first, second):
    first_new = BETA_ONE * first + (1.0 - BETA_ONE) * gradient
    second_new = BETA_TWO * second + (1.0 - BETA_TWO) * gradient * gradient
    first_hat = first_new / (1.0 - BETA_ONE**ADAM_STEP)
    second_hat = second_new / (1.0 - BETA_TWO**ADAM_STEP)
    return (master - RATE * first_hat / (jnp.sqrt(second_hat) + EPSILON), first_new, second_new)


def source_total(pieces):
    head_width = pieces.shape[2]
    item_count = pieces.shape[1]
    summed = (
        pieces.astype(jnp.float32)
        .reshape(KV, pieces.shape[0] // KV, item_count, head_width)
        .sum(axis=1)
    )
    return summed.transpose(1, 0, 2).reshape(item_count, KV * head_width)


def totals_pair(pieces):
    return (source_total(pieces[0]), source_total(pieces[1]))


def per_device(
    hidden,
    out_grad,
    norm_gain,
    w_query,
    w_key,
    w_value,
    w_out,
    cache_keys,
    cache_values,
    first_moment,
    second_moment,
    conv_lengths,
    row_offsets,
):
    cache_count = lax.axis_size("cache")
    data_count = lax.axis_size("dp")
    pos_count = cache_keys.shape[0]
    device_count = cache_count * data_count
    cache_len = pos_count * device_count
    head_width = w_query.shape[1]
    column_share = w_key.shape[2]
    groups = cache_count // KV
    kv_head = lax.axis_index("cache") // groups
    score_scale = head_width ** (-0.5)
    hidden_full, grad_full = (
        lax.all_gather(hidden, "cache", axis=1, tiled=True),
        lax.all_gather(out_grad, "cache", axis=1, tiled=True),
    )
    row_count = hidden_full.shape[0]
    width_full = hidden_full.shape[1]
    hidden_f = hidden_full.astype(jnp.float32)
    inv_rms = lax.rsqrt(jnp.mean(hidden_f * hidden_f, axis=1, keepdims=True) + 1e-05)
    normed = (hidden_f * inv_rms * norm_gain).astype(jnp.bfloat16)
    segment, position = row_layout(conv_lengths[0], row_offsets[0], row_count, cache_len)
    cos_table, sin_table = rope_tables(position, head_width)
    query = rotate(
        jnp.dot(normed, w_query, preferred_element_type=jnp.float32), cos_table, sin_table
    ).astype(jnp.bfloat16)
    key_piece = (
        jnp.dot(
            normed, w_key.reshape(width_full, KV * column_share), preferred_element_type=jnp.float32
        )
        .astype(jnp.bfloat16)
        .reshape(row_count, KV, column_share)
    )
    value_piece = (
        jnp.dot(
            normed,
            w_value.reshape(width_full, KV * column_share),
            preferred_element_type=jnp.float32,
        )
        .astype(jnp.bfloat16)
        .reshape(row_count, KV, column_share)
    )
    keys_raw, values_self = (
        lax.all_gather(key_piece, "cache", axis=2, tiled=True),
        lax.all_gather(value_piece, "cache", axis=2, tiled=True),
    )
    own_keys = lax.dynamic_slice_in_dim(keys_raw, kv_head, 1, 1).reshape(row_count, head_width)
    self_k = rotate(own_keys.astype(jnp.float32), cos_table, sin_table).astype(jnp.bfloat16)
    self_v = lax.dynamic_slice_in_dim(values_self, kv_head, 1, 1).reshape(row_count, head_width)
    grad_out = lax.dot_general(
        grad_full, w_out, (((1,), (1,)), ((), ())), preferred_element_type=jnp.float32
    ).astype(jnp.bfloat16)
    cache_k = cache_keys.astype(jnp.bfloat16)
    cache_v = cache_values.astype(jnp.bfloat16)
    keys_all, values_all = (
        lax.all_gather(cache_k, ("cache", "dp"), axis=0, tiled=True),
        lax.all_gather(cache_v, ("cache", "dp"), axis=0, tiled=True),
    )
    head_k = lax.dynamic_slice_in_dim(keys_all, kv_head * head_width, head_width, 1)
    head_v = lax.dynamic_slice_in_dim(values_all, kv_head * head_width, head_width, 1)
    row_index = jnp.arange(row_count, dtype=jnp.int32)
    allowed = (segment[:, None] == segment[None, :]) & (row_index[None, :] <= row_index[:, None])
    grad_score, weight_cache = attend(
        query, grad_out, head_k, head_v, self_k, self_v, allowed, score_scale
    )
    transposed = (((0,), (0,)), ((), ()))
    key_part = (
        lax.dot_general(grad_score, query, transposed, preferred_element_type=jnp.float32)
        * score_scale
    ).astype(jnp.bfloat16)
    value_part = lax.dot_general(
        weight_cache, grad_out, transposed, preferred_element_type=jnp.float32
    ).astype(jnp.bfloat16)
    send_k = key_part.reshape(device_count, pos_count, head_width)
    send_v = value_part.reshape(device_count, pos_count, head_width)
    grad_k, grad_v = totals_pair(
        (
            lax.all_to_all(send_k, ("cache", "dp"), split_axis=0, concat_axis=0, tiled=True),
            lax.all_to_all(send_v, ("cache", "dp"), split_axis=0, concat_axis=0, tiled=True),
        )
    )
    gradient = jnp.stack([grad_k, grad_v])
    master = jnp.stack([cache_keys, cache_values])
    new_master, first_new, second_new = adam_update(master, gradient, first_moment, second_moment)
    return (new_master[0], new_master[1], first_new, second_new)


def solution(mesh):
    return jax.shard_map(
        per_device,
        mesh=mesh,
        in_specs=(
            P(("groups", "dp"), "cache"),
            P(("groups", "dp"), "cache"),
            P(),
            P(None, "cache"),
            P(None, None, "cache"),
            P(None, None, "cache"),
            P("cache", None),
            P(("groups", "cache", "dp"), None),
            P(("groups", "cache", "dp"), None),
            P(None, ("groups", "cache", "dp"), None),
            P(None, ("groups", "cache", "dp"), None),
            P(("groups", "dp"), None),
            P(("groups", "dp"), None),
        ),
        out_specs=(
            P(("groups", "cache", "dp"), None),
            P(("groups", "cache", "dp"), None),
            P(None, ("groups", "cache", "dp"), None),
            P(None, ("groups", "cache", "dp"), None),
        ),
        check_vma=False,
    )
```

profile of v0, /device:TPU:13, one launch (start us, length us, event | category | flops | bytes accessed | tf_op | source)
XLA Modules:
  0.0 355.9 jit_solution(13640633634136398060)
XLA Ops:
  8.0 1.5 convert_element_type.63
  10.3 1.5 convert_element_type.68
  14.3 86.4 %all-gather.5.cloned.1.call-done = bf16[320,8192]{1,0:T(8,128)(2,1)} async-done(((bf16[320,512]{1,0:T(8,128)(2,1)}), bf16[320,8192]{1,0:T(8,128)(2,1)}) %all-gather.5.cloned.1.call-update) | async-done | bytes 5242896 | tf_op jit(solution)/shard_map/all_gather | solution.py:131
  100.6 3.8 %fusion = f32[320]{0:T(512)S(1)} fusion(bf16[320,8192]{1,0:T(8,128)(2,1)} %all-gather.5.cloned.1.call-done), kind=kLoop, calls=%fused_computation.2 | loop fusion | flops 7864000 | bytes 5244160 | tf_op jit(solution)/shard_map/reduce_sum | solution.py:137
  104.7 1.6 fusion.2
  106.3 1.6 fusion.13
  108.7 31.9 %all_gather.20 = bf16[320,8,128]{0,1,2:T(8,128)(2,1)S(1)} all-gather(bf16[320,8,8]{0,1,2:T(8,128)(2,1)S(1)} %copy.24), channel_id=1, replica_groups=mesh['groups'=1,'cache'=16,'dp'=2] {'cache'}, dimensions={2}, use_global_device_ids=true | all-gather | bytes 696320 | tf_op jit(solution)/shard_map/all_gather | solution.py:161
  141.0 4.0 %fusion.59 = f32[320,128]{1,0:T(8,128)S(1)} fusion(bf16[320,8192]{1,0:T(8,128)(2,1)} %copy-done.1, bf16[8192,128]{1,0:T(8,128)(2,1)S(1)} %copy-done), kind=kOutput, calls=%fused_computation.93 | convolution fusion | flops 671088640 | bytes 7503872 | tf_op jit(solution)/shard_map/dot_general | solution.py:142
  145.8 16.0 %all-gather.7.cloned.1.call-done = bf16[1024,1024]{1,0:T(8,128)(2,1)} async-done(((bf16[32,1024]{1,0:T(8,128)(2,1)}), bf16[1024,1024]{1,0:T(8,128)(2,1)}) %all-gather.7.cloned.1.call-update) | async-done | bytes 2097168 | tf_op jit(solution)/shard_map/all_gather | solution.py:173
  161.8 1.5 fusion.57
  164.2 4.1 %fusion.14 = bf16[320,8,8]{0,2,1:T(8,128)(2,1)S(1)} fusion(bf16[320,8192]{1,0:T(8,128)(2,1)} %copy-done.1, bf16[8192,8,8]{0,2,1:T(8,128)(2,1)S(1)} %copy-done.4), kind=kOutput, calls=%fused_computation.25 | convolution fusion | flops 335564800 | bytes 6332416 | tf_op jit(solution)/shard_map/dot_general | solution.py:152
  168.3 35.0 %all_gather.23 = bf16[320,8,128]{0,2,1:T(8,128)(2,1)S(1)} all-gather(bf16[320,8,8]{0,2,1:T(8,128)(2,1)S(1)} %fusion.14), channel_id=1, replica_groups=mesh['groups'=1,'cache'=16,'dp'=2] {'cache'}, dimensions={2}, use_global_device_ids=true | all-gather | bytes 696320 | tf_op jit(solution)/shard_map/all_gather | solution.py:162
  204.6 52.8 %all-gather.9.cloned.1.call-done = bf16[320,8192]{1,0:T(8,128)(2,1)} async-done(((bf16[320,512]{1,0:T(8,128)(2,1)}), bf16[320,8192]{1,0:T(8,128)(2,1)}) %all-gather.9.cloned.1.call-update) | async-done | bytes 5242896 | tf_op jit(solution)/shard_map/all_gather | solution.py:132
  257.4 4.7 %convolution_convert_fusion.1 = bf16[320,128]{1,0:T(8,128)(2,1)S(1)} fusion(bf16[320,8192]{1,0:T(8,128)(2,1)} %all-gather.9.cloned.1.call-done, bf16[128,8192]{1,0:T(8,128)(2,1)} %param.19), kind=kOutput, calls=%fused_computation.20 | convolution fusion | flops 671129600 | bytes 7421952 | tf_op jit(solution)/shard_map/dot_general | solution.py:167
  262.1 55.0 %all-gather.11.cloned.1.call-done = bf16[1024,1024]{1,0:T(8,128)(2,1)} async-done(((bf16[32,1024]{1,0:T(8,128)(2,1)}), bf16[1024,1024]{1,0:T(8,128)(2,1)}) %all-gather.11.cloned.1.call-update) | async-done | bytes 2097168 | tf_op jit(solution)/shard_map/all_gather | solution.py:174
  317.1 1.4 fusion.12
  318.5 2.5 fusion.8
  321.0 4.6 %all-to-all-start = ((bf16[32,32,128]{2,1,0:T(8,128)(2,1)}), bf16[32,32,128]{2,1,0:T(8,128)(2,1)}, u32[]{:S(2)}, u32[]{:S(2)}) async-start(bf16[32,32,128]{2,1,0:T(8,128)(2,1)} %bitcast.50), calls=%async_computation | async-start | bytes 524288 | tf_op jit(solution)/shard_map/all_to_all | solution.py:195
  325.6 1.1 convolution_convert_fusion
  326.7 7.6 %all-to-all-done = bf16[32,32,128]{2,1,0:T(8,128)(2,1)} async-done(((bf16[32,32,128]{2,1,0:T(8,128)(2,1)}), bf16[32,32,128]{2,1,0:T(8,128)(2,1)}, u32[]{:S(2)}, u32[]{:S(2)}) %all-to-all-start) | async-done | bytes 262176 | tf_op jit(solution)/shard_map/all_to_all | solution.py:195
  334.3 4.4 %all-to-all-start.1 = ((bf16[32,32,128]{2,1,0:T(8,128)(2,1)}), bf16[32,32,128]{2,1,0:T(8,128)(2,1)S(1)}, u32[]{:S(2)}, u32[]{:S(2)}) async-start(bf16[32,32,128]{2,1,0:T(8,128)(2,1)} %bitcast.49), calls=%async_computation.1 | async-start | bytes 524288 | tf_op jit(solution)/shard_map/all_to_all | solution.py:196
  338.7 1.0 convert_reduce_fusion.1
  339.9 7.6 %all-to-all-done.1 = bf16[32,32,128]{2,1,0:T(8,128)(2,1)S(1)} async-done(((bf16[32,32,128]{2,1,0:T(8,128)(2,1)}), bf16[32,32,128]{2,1,0:T(8,128)(2,1)S(1)}, u32[]{:S(2)}, u32[]{:S(2)}) %all-to-all-start.1) | async-done | bytes 262176 | tf_op jit(solution)/shard_map/all_to_all | solution.py:196
  347.7 1.0 maximum_subtract_fusion
  (59 shorter events, 9.1 us)
Async XLA Ops:
  7.2 133.8 %copy-start = (bf16[8192,128]{1,0:T(8,128)(2,1)S(1)}, bf16[8192,128]{1,0:T(8,128)(2,1)}, u32[]{:S(2)}) copy-start(bf16[8192,128]{1,0:T(8,128)(2,1)} %param.16) | copy-start | bytes 6291460
  7.2 93.5 %all-gather.5.cloned.1.call-start = ((), (), s32[]{:S(2)}) async-start(), calls=%async_computation.2 | async-start | bytes 5570560 | tf_op jit(solution)/shard_map/all_gather | solution.py:131
  7.9 153.9 %all-gather.7.cloned.1.call-start = ((), (), s32[]{:S(2)}) async-start(), calls=%async_computation.3 | async-start | bytes 2162688 | tf_op jit(solution)/shard_map/all_gather | solution.py:173
  9.5 247.9 %all-gather.9.cloned.1.call-start = ((), (), s32[]{:S(2)}) async-start(), calls=%async_computation.4 | async-start | bytes 5570560 | tf_op jit(solution)/shard_map/all_gather | solution.py:132
  10.3 306.8 %all-gather.11.cloned.1.call-start = ((), (), s32[]{:S(2)}) async-start(), calls=%async_computation.5 | async-start | bytes 2162688 | tf_op jit(solution)/shard_map/all_gather | solution.py:174
  11.9 92.5 %copy-start.11 = (f32[8192]{0:T(1024)S(1)}, f32[8192]{0:T(1024)}, u32[]{:S(2)}) copy-start(f32[8192]{0:T(1024)} %param.15) | copy-start | bytes 98308
  100.6 4.0 %copy-start.2 = (bf16[320,8192]{1,0:T(8,128)(2,1)S(1)}, bf16[320,8192]{1,0:T(8,128)(2,1)}, u32[]{:S(2)}) copy-start(bf16[320,8192]{1,0:T(8,128)(2,1)} %all-gather.5.cloned.1.call-done) | copy-start | bytes 15728644
  104.7 1.6 copy-start.3
  106.3 2.3 copy-start.1
  145.7 18.4 %copy-start.5 = (bf16[320,64]{1,0:T(8,128)(2,1)}, bf16[320,64]{1,0:T(8,128)(2,1)S(1)}, u32[]{:S(2)}) copy-start(bf16[320,64]{1,0:T(8,128)(2,1)S(1)} %get-tuple-element.15) | copy-start | bytes 122884
  145.7 18.4 %copy-start.6 = (bf16[320,64]{1,0:T(8,128)(2,1)}, bf16[320,64]{1,0:T(8,128)(2,1)S(1)}, u32[]{:S(2)}) copy-start(bf16[320,64]{1,0:T(8,128)(2,1)S(1)} %get-tuple-element.16) | copy-start | bytes 122884
  161.8 2.4 copy-start.4
  321.0 13.4 %all-to-all-start = ((bf16[32,32,128]{2,1,0:T(8,128)(2,1)}), bf16[32,32,128]{2,1,0:T(8,128)(2,1)}, u32[]{:S(2)}, u32[]{:S(2)}) async-start(bf16[32,32,128]{2,1,0:T(8,128)(2,1)} %bitcast.50), calls=%async_computation | async-start | bytes 524288 | tf_op jit(solution)/shard_map/all_to_all | solution.py:195
  326.7 21.0 %copy-start.7 = (f32[32,1024]{1,0:T(8,128)S(1)}, f32[32,1024]{1,0:T(8,128)}, u32[]{:S(2)}) copy-start(f32[32,1024]{1,0:T(8,128)} %param.21) | copy-start | bytes 393220
  326.7 21.0 %copy-start.8 = (f32[32,1024]{1,0:T(8,128)S(1)}, f32[32,1024]{1,0:T(8,128)}, u32[]{:S(2)}) copy-start(f32[32,1024]{1,0:T(8,128)} %param.20) | copy-start | bytes 393220
  326.7 21.0 %copy-start.9 = (f32[2,32,1024]{2,1,0:T(8,128)S(1)}, f32[2,32,1024]{2,1,0:T(8,128)}, u32[]{:S(2)}) copy-start(f32[2,32,1024]{2,1,0:T(8,128)} %param.22) | copy-start | bytes 786436
  326.7 21.1 %copy-start.10 = (f32[2,32,1024]{2,1,0:T(8,128)S(1)}, f32[2,32,1024]{2,1,0:T(8,128)}, u32[]{:S(2)}) copy-start(f32[2,32,1024]{2,1,0:T(8,128)} %param.23) | copy-start | bytes 786436
  334.3 13.2 %all-to-all-start.1 = ((bf16[32,32,128]{2,1,0:T(8,128)(2,1)}), bf16[32,32,128]{2,1,0:T(8,128)(2,1)S(1)}, u32[]{:S(2)}, u32[]{:S(2)}) async-start(bf16[32,32,128]{2,1,0:T(8,128)(2,1)} %bitcast.49), calls=%async_computation.1 | async-start | bytes 524288 | tf_op jit(solution)/shard_map/all_to_all | solution.py:196
Sparse Core Ops, SparseCore 0:
  10.7 89.8 all-gather.4
  104.1 57.6 all-gather.6
  164.5 92.8 all-gather.8
  260.7 56.3 all-gather.10
where the time goes:
time: 359 us; the launch traced here: 356 us
  waiting for transfers between devices  227 us (63%)
  blocking collectives  66.9 us (19%)
  matrix products  22.2 us (6%)
  other arithmetic  14.4 us (4%)
  between operations  14.1 us (4%)
  starting transfers between devices  9.15 us (3%)
    all_gather x1, waiting for transfers between devices, per_device(): lax.all_gather(hidden, 'cache', axis=1, tiled=True)  86.4 us
    all_gather x1, waiting for transfers between devices, per_device(): lax.all_gather(cache_v, ('cache', 'dp'), axis=0, tiled=True)  55 us
    all_gather x1, waiting for transfers between devices, per_device(): lax.all_gather(out_grad, 'cache', axis=1, tiled=True)  52.8 us
    all_gather x1, blocking collectives, per_device(): lax.all_gather(value_piece, 'cache', axis=2, tiled=True)  35 us
    all_gather x1, blocking collectives, per_device(): lax.all_gather(key_piece, 'cache', axis=2, tiled=True)  31.9 us
    all_gather x1, waiting for transfers between devices, per_device(): lax.all_gather(cache_k, ('cache', 'dp'), axis=0, tiled=True)  16 us
    all_to_all x1, waiting for transfers between devices, per_device(): lax.all_to_all(send_k, ('cache', 'dp'), split_axis=0, concat_axis=0, tile...  7.64 us
    all_to_all x1, waiting for transfers between devices, per_device(): lax.all_to_all(send_v, ('cache', 'dp'), split_axis=0, concat_axis=0, tile...  7.63 us
  transfers between devices with their start and end apart: 6, of which 6 were waited for; matrix products, arithmetic and copies ran while one was open for 9% of the time, Pallas kernels for 0%

commit v1 on v0

--- a/solution.py
+++ b/solution.py
@@ -3,6 +3,8 @@
 import jax
 import jax.numpy as jnp
 from jax import lax
+from jax.experimental import pallas as pl
+from jax.experimental.pallas import tpu as pltpu
 from jax.sharding import PartitionSpec as P
 
 KV = 8
@@ -202,9 +204,535 @@
     return (new_master[0], new_master[1], first_new, second_new)
 
 
+LINE = 4
+PLANE = 4
+MESH = pl.DeviceIdType.MESH
+
+
+def fits(mesh):
+    return mesh.shape["cache"] == LINE * PLANE and mesh.shape["dp"] == 2
+
+
+def fused_kernel(
+    hid,
+    og,
+    ss_in,
+    gain,
+    wqkv,
+    wout,
+    ckv,
+    cosd,
+    sind,
+    cos_t,
+    sin_t,
+    mask_t,
+    eye,
+    ck,
+    cv,
+    fm,
+    sm,
+    nk,
+    nv,
+    nf,
+    ns,
+    hbuf,
+    obuf,
+    srecv,
+    wbuf,
+    wobuf,
+    cbuf,
+    cpart,
+    crecv,
+    dpart,
+    drecv,
+    kvt,
+    kvr,
+    gsend,
+    grecv,
+    h_s,
+    h_r,
+    o_s,
+    o_r,
+    s_s,
+    s_r,
+    w_s,
+    w_r,
+    wf_s,
+    wf_r,
+    wo_s,
+    wo_r,
+    wof_s,
+    wof_r,
+    c_s,
+    c_r,
+    rc_s,
+    rc_r,
+    rd_s,
+    rd_r,
+    kv_s,
+    kv_r,
+    g_s,
+    g_r,
+    loc,
+    loco,
+):
+    chips = LINE * PLANE
+    devs = 2 * chips
+    m = lax.axis_index("cache")
+    c = lax.axis_index("dp")
+    i = m * 2 + c
+    line, p = m // PLANE, m % PLANE
+    width = hid.shape[1]
+    pair = LINE // 2
+    mine = c * pair
+    other = (1 - c) * pair
+    f32, bf16 = jnp.float32, jnp.bfloat16
+
+    barrier = pltpu.get_barrier_semaphore()
+
+    def greet(k, carry):
+        j = (i + k) % devs
+        pl.semaphore_signal(
+            barrier, inc=1, device_id={"cache": j // 2, "dp": j % 2}, device_id_type=MESH
+        )
+        return carry
+
+    lax.fori_loop(1, devs, greet, 0)
+
+    own_w = pltpu.make_async_copy(wqkv.at[:, p], wbuf.at[0], loc.at[0])
+    own_w.start()
+    own_wo = []
+    for zz in range(LINE):
+        col = pl.multiple_of((zz * PLANE + p) * width, width)
+        cp = pltpu.make_async_copy(wout.at[:, pl.ds(col, width)], wobuf.at[0, zz], loco.at[zz])
+        cp.start()
+        own_wo.append(cp)
+    own_c = pltpu.make_async_copy(ckv.at[m // (chips // KV)], cbuf.at[i], loc.at[1])
+    own_c.start()
+    pl.semaphore_wait(barrier, devs - 1)
+
+    def remote(src, dst, ss, rs, chip, core):
+        return pltpu.make_async_remote_copy(
+            src_ref=src,
+            dst_ref=dst,
+            send_sem=ss,
+            recv_sem=rs,
+            device_id={"cache": chip, "dp": core},
+            device_id_type=MESH,
+        )
+
+    def ss_copy(k):
+        return remote(ss_in, srecv.at[k], s_s.at[k], s_r.at[k], (m + k) % chips, c)
+
+    def start_ss(k, carry):
+        ss_copy(k).start()
+        return carry
+
+    lax.fori_loop(1, chips, start_ss, 0)
+
+    def line_chip(k):
+        return ((line + k) % LINE) * PLANE + p
+
+    def plane_chip(k):
+        return line * PLANE + (p + k) % PLANE
+
+    def back_chip(k):
+        return line * PLANE + (p + PLANE - k) % PLANE
+
+    o_cp, h_cp, w_cp, wo_cp = {}, {}, {}, {}
+    for k in range(1, LINE):
+        o_cp[k] = remote(og, obuf.at[k], o_s.at[k], o_r.at[k], line_chip(k), c)
+        o_cp[k].start()
+    for k in range(1, PLANE):
+        for h in range(pair):
+            col = pl.multiple_of(((mine + h) * PLANE + (p + k) % PLANE) * width, width)
+            wo_cp[k, h] = remote(
+                wout.at[:, pl.ds(col, width)],
+                wobuf.at[k, mine + h],
+                wo_s.at[k, h],
+                wo_r.at[k, h],
+                plane_chip(k),
+                c,
+            )
+            wo_cp[k, h].start()
+    for k in range(1, LINE):
+        h_cp[k] = remote(hid, hbuf.at[k], h_s.at[k], h_r.at[k], line_chip(k), c)
+        h_cp[k].start()
+    for k in range(1, PLANE):
+        w_cp[k] = remote(
+            wqkv.at[pl.ds(mine, pair), (p + k) % PLANE],
+            wbuf.at[k, pl.ds(mine, pair)],
+            w_s.at[k],
+            w_r.at[k],
+            plane_chip(k),
+            c,
+        )
+        w_cp[k].start()
+
+    def c_copy(k):
+        j = (i + k) % devs
+        return remote(
+            ckv.at[(j // 2) // (chips // KV)], cbuf.at[i], c_s.at[k], c_r.at[k], j // 2, j % 2
+        )
+
+    def start_c(k, carry):
+        c_copy(k).start()
+        return carry
+
+    lax.fori_loop(1, devs, start_c, 0)
+
+    wof_cp = {}
+    for k in range(1, PLANE):
+        for h in range(pair):
+            wo_cp[k, h].wait_recv()
+            wof_cp[k, h] = remote(
+                wobuf.at[k, mine + h],
+                wobuf.at[k, mine + h],
+                wof_s.at[k, h],
+                wof_r.at[k, h],
+                m,
+                1 - c,
+            )
+            wof_cp[k, h].start()
+    for cp in own_wo:
+        cp.wait()
+    for k in range(1, PLANE):
+        for h in range(pair):
+            wof_cp[k, h].wait_recv()
+
+    for kz in range(LINE):
+        if kz == 0:
+            block = og[...]
+        else:
+            o_cp[kz].wait_recv()
+            block = obuf[kz]
+        zz = (line + LINE - kz) % LINE
+
+        def add_d(k, carry):
+            term = lax.dot_general(
+                block, wobuf[k, zz], (((1,), (1,)), ((), ())), preferred_element_type=f32
+            )
+            if kz == 0:
+                dpart[k] = term
+            else:
+                dpart[k] = dpart[k] + term
+            return carry
+
+        lax.fori_loop(0, PLANE, add_d, 0)
+
+    rd_cp = {}
+    for k in range(1, PLANE):
+        rd_cp[k] = remote(dpart.at[k], drecv.at[k], rd_s.at[k], rd_r.at[k], back_chip(k), c)
+        rd_cp[k].start()
+
+    wf_cp = {}
+    for k in range(1, PLANE):
+        w_cp[k].wait_recv()
+        part = wbuf.at[k, pl.ds(mine, pair)]
+        wf_cp[k] = remote(part, part, wf_s.at[k], wf_r.at[k], m, 1 - c)
+        wf_cp[k].start()
+
+    def wait_ss(k, carry):
+        ss_copy(k).wait()
+        return carry
+
+    lax.fori_loop(1, chips, wait_ss, 0)
+    srecv[0] = ss_in[...]
+    total = jnp.sum(srecv[...], axis=0)
+    spread = lax.dot_general(
+        total,
+        jnp.full((8, 128), 0.125, f32),
+        (((0,), (0,)), ((), ())),
+        preferred_element_type=f32,
+        precision=lax.Precision.HIGHEST,
+    )
+    inv = lax.rsqrt(spread[:, :1] * (1.0 / (width * chips)) + 1e-05)
+    own_w.wait()
+    for k in range(1, PLANE):
+        wf_cp[k].wait_recv()
+    for kz in range(LINE):
+        zz = (line + LINE - kz) % LINE
+        if kz == 0:
+            block = hid[...]
+        else:
+            h_cp[kz].wait_recv()
+            block = hbuf[kz]
+        normed = (block.astype(f32) * inv * gain[zz * PLANE + p]).astype(bf16)
+
+        def add_c(k, carry):
+            term = jnp.dot(normed, wbuf[k, zz], preferred_element_type=f32)
+            if kz == 0:
+                cpart[k] = term
+            else:
+                cpart[k] = cpart[k] + term
+            return carry
+
+        lax.fori_loop(0, PLANE, add_c, 0)
+
+    rc_cp = {}
+    for k in range(1, PLANE):
+        rc_cp[k] = remote(cpart.at[k], crecv.at[k], rc_s.at[k], rc_r.at[k], back_chip(k), c)
+        rc_cp[k].start()
+
+    grad = dpart[0]
+    for k in range(1, PLANE):
+        rd_cp[k].wait_recv()
+        grad = grad + drecv[k]
+    grad = grad.astype(bf16)
+    grad_t = lax.dot_general(
+        eye[...], grad, (((1,), (1,)), ((), ())), preferred_element_type=f32
+    )
+    own_c.wait()
+
+    def wait_c(k, carry):
+        c_copy(k).wait()
+        return carry
+
+    lax.fori_loop(1, devs, wait_c, 0)
+    rows = ck.shape[0]
+    cache_len = rows * devs
+    head_k = cbuf[:, :rows, :].reshape(cache_len, 128)
+    head_v = cbuf[:, rows:, :].reshape(cache_len, 128)
+    grad_prob = lax.dot_general(
+        head_v, grad, (((1,), (1,)), ((), ())), preferred_element_type=f32
+    )
+
+    qkv = cpart[0]
+    for k in range(1, PLANE):
+        rc_cp[k].wait_recv()
+        qkv = qkv + crecv[k]
+    kv = qkv[:, 128:].astype(bf16)
+    kvt[...] = lax.dot_general(
+        eye[...], kv, (((1,), (1,)), ((), ())), preferred_element_type=f32
+    ).astype(bf16)
+
+    def kv_part(chip):
+        return kvt.at[pl.ds(pl.multiple_of((chip // (chips // KV)) * 16, 16), 16)]
+
+    def kv_copy(k):
+        j = (m + k) % chips
+        return remote(kv_part(j), kvr.at[m], kv_s.at[k], kv_r.at[k], j, c)
+
+    def start_kv(k, carry):
+        kv_copy(k).start()
+        return carry
+
+    lax.fori_loop(1, chips, start_kv, 0)
+    own_kv = pltpu.make_async_copy(kv_part(m), kvr.at[m], loc.at[2])
+    own_kv.start()
+
+    scale = 128 ** (-0.5)
+    q_raw = qkv[:, :128]
+    turned = jnp.concatenate([q_raw[:, 64:], q_raw[:, :64]], axis=1)
+    query = (q_raw * cosd[...] + turned * sind[...]).astype(bf16)
+    query_t = lax.dot_general(
+        eye[...], query, (((1,), (1,)), ((), ())), preferred_element_type=f32
+    ).astype(bf16)
+    score = jnp.dot(head_k, query_t, preferred_element_type=f32) * scale
+    top = jnp.max(score, axis=0, keepdims=True)
+
+    def wait_kv(k, carry):
+        kv_copy(k).wait()
+        return carry
+
+    lax.fori_loop(1, chips, wait_kv, 0)
+    own_kv.wait()
+    kvf = kvr[...].astype(f32)
+    key_t = kvf[:, :8, :].reshape(128, kvf.shape[2])
+    value_t = kvf[:, 8:, :].reshape(128, kvf.shape[2]).astype(bf16)
+    turned_t = jnp.concatenate([key_t[64:], key_t[:64]], axis=0)
+    key_t = (key_t * cos_t[...] + turned_t * sin_t[...]).astype(bf16)
+    score_self = (
+        lax.dot_general(key_t, query_t, (((0,), (0,)), ((), ())), preferred_element_type=f32)
+        * scale
+    )
+    score_self = jnp.where(mask_t[...] > 0.5, score_self, -1e30)
+    top = jnp.maximum(top, jnp.max(score_self, axis=0, keepdims=True))
+    e_cache = jnp.exp(score - top)
+    e_self = jnp.exp(score_self - top)
+    inverse = 1.0 / (
+        jnp.sum(e_cache, axis=0, keepdims=True) + jnp.sum(e_self, axis=0, keepdims=True)
+    )
+    prob = e_cache * inverse
+    weight = prob.astype(bf16)
+    weight_self = (e_self * inverse).astype(bf16)
+    attended = lax.dot_general(
+        head_v, weight, (((0,), (0,)), ((), ())), preferred_element_type=f32
+    ) + jnp.dot(value_t, weight_self, preferred_element_type=f32)
+    delta = jnp.sum(grad_t * attended, axis=0, keepdims=True)
+    grad_score = (prob * (grad_prob - delta)).astype(bf16)
+    value_part = jnp.dot(weight, grad, preferred_element_type=f32).astype(bf16)
+    key_part = (jnp.dot(grad_score, query, preferred_element_type=f32) * scale).astype(bf16)
+    gsend[:, :rows, :] = key_part.reshape(devs, rows, 128)
+    gsend[:, rows:, :] = value_part.reshape(devs, rows, 128)
+
+    def g_copy(k):
+        j = (i + k) % devs
+        return remote(gsend.at[j], grecv.at[i], g_s.at[k], g_r.at[k], j // 2, j % 2)
+
+    def start_g(k, carry):
+        g_copy(k).start()
+        return carry
+
+    lax.fori_loop(1, devs, start_g, 0)
+    own_g = pltpu.make_async_copy(gsend.at[i], grecv.at[i], loc.at[3])
+    own_g.start()
+
+    for k in range(1, LINE):
+        o_cp[k].wait_send()
+        h_cp[k].wait_send()
+    for k in range(1, PLANE):
+        w_cp[k].wait_send()
+        wf_cp[k].wait_send()
+        rd_cp[k].wait_send()
+        rc_cp[k].wait_send()
+        for h in range(pair):
+            wo_cp[k, h].wait_send()
+            wof_cp[k, h].wait_send()
+
+    def wait_g(k, carry):
+        g_copy(k).wait()
+        return carry
+
+    lax.fori_loop(1, devs, wait_g, 0)
+    own_g.wait()
+
+    share = devs // KV
+    for g in range(KV):
+        got = jnp.sum(grecv[g * share : (g + 1) * share].astype(f32), axis=0)
+        cols = slice(g * 128, (g + 1) * 128)
+        for which, master, out in ((0, ck, nk), (1, cv, nv)):
+            gradient = got[which * rows : (which + 1) * rows]
+            new, first, second = adam_update(
+                master[:, cols], gradient, fm[which, :, cols], sm[which, :, cols]
+            )
+            out[:, cols] = new
+            nf[which, :, cols] = first
+            ns[which, :, cols] = second
+
+
+def fused_device(
+    hidden,
+    out_grad,
+    norm_gain,
+    w_query,
+    w_key,
+    w_value,
+    w_out,
+    cache_keys,
+    cache_values,
+    first_moment,
+    second_moment,
+    conv_lengths,
+    row_offsets,
+):
+    chips = LINE * PLANE
+    devs = 2 * chips
+    f32, bf16 = jnp.float32, jnp.bfloat16
+    rows, width = hidden.shape
+    pos = cache_keys.shape[0]
+    cache_len = pos * devs
+    head = w_query.shape[1]
+    full = w_query.shape[0]
+    hf = hidden.astype(f32)
+    squares = jnp.broadcast_to(jnp.sum(hf * hf, axis=1)[None, :], (8, rows))
+    w_kv = jnp.stack([w_key, w_value], axis=2).reshape(full, head)
+    wqkv = jnp.concatenate([w_query, w_kv], axis=1).reshape(LINE, PLANE, width, 2 * head)
+    ckv = jnp.stack(
+        [cache_keys.astype(bf16).reshape(pos, KV, head), cache_values.astype(bf16).reshape(pos, KV, head)]
+    )
+    ckv = ckv.transpose(2, 0, 1, 3).reshape(KV, 2 * pos, head)
+    segment, position = row_layout(conv_lengths[0], row_offsets[0], rows, cache_len)
+    cos, sin = rope_tables(position, head)
+    cosd = jnp.concatenate([cos, cos], axis=1)
+    sind = jnp.concatenate([-sin, sin], axis=1)
+    index = jnp.arange(rows, dtype=jnp.int32)
+    mask_t = ((segment[:, None] == segment[None, :]) & (index[:, None] <= index[None, :])).astype(f32)
+    eye = jnp.eye(head, dtype=bf16)
+    vm = pl.BlockSpec(memory_space=pltpu.VMEM)
+    hbm = pl.BlockSpec(memory_space=pl.ANY)
+    dma = pltpu.SemaphoreType.DMA
+    pair = LINE // 2
+    out_shape = (
+        jax.ShapeDtypeStruct(cache_keys.shape, f32),
+        jax.ShapeDtypeStruct(cache_keys.shape, f32),
+        jax.ShapeDtypeStruct(first_moment.shape, f32),
+        jax.ShapeDtypeStruct(first_moment.shape, f32),
+    )
+    return pl.pallas_call(
+        fused_kernel,
+        out_shape=out_shape,
+        in_specs=[vm, vm, vm, vm, hbm, hbm] + [vm] * 11,
+        out_specs=(vm,) * 4,
+        scratch_shapes=[
+            pltpu.VMEM((LINE, rows, width), bf16),
+            pltpu.VMEM((LINE, rows, width), bf16),
+            pltpu.VMEM((chips, 8, rows), f32),
+            pltpu.VMEM((PLANE, LINE, width, 2 * head), bf16),
+            pltpu.VMEM((PLANE, LINE, head, width), bf16),
+            pltpu.VMEM((devs, 2 * pos, head), bf16),
+            pltpu.VMEM((PLANE, rows, 2 * head), f32),
+            pltpu.VMEM((PLANE, rows, 2 * head), f32),
+            pltpu.VMEM((PLANE, rows, head), f32),
+            pltpu.VMEM((PLANE, rows, head), f32),
+            pltpu.VMEM((head, rows), bf16),
+            pltpu.VMEM((chips, 16, rows), bf16),
+            pltpu.VMEM((devs, 2 * pos, head), bf16),
+            pltpu.VMEM((devs, 2 * pos, head), bf16),
+            dma((LINE,)),
+            dma((LINE,)),
+            dma((LINE,)),
+            dma((LINE,)),
+            dma((chips,)),
+            dma((chips,)),
+            dma((PLANE,)),
+            dma((PLANE,)),
+            dma((PLANE,)),
+            dma((PLANE,)),
+            dma((PLANE, pair)),
+            dma((PLANE, pair)),
+            dma((PLANE, pair)),
+            dma((PLANE, pair)),
+            dma((devs,)),
+            dma((devs,)),
+            dma((PLANE,)),
+            dma((PLANE,)),
+            dma((PLANE,)),
+            dma((PLANE,)),
+            dma((chips,)),
+            dma((chips,)),
+            dma((devs,)),
+            dma((devs,)),
+            dma((4,)),
+            dma((LINE,)),
+        ],
+        compiler_params=pltpu.CompilerParams(
+            collective_id=0, has_side_effects=True, vmem_limit_bytes=56 * 1024 * 1024
+        ),
+    )(
+        hidden,
+        out_grad,
+        squares,
+        norm_gain.reshape(chips, 1, width),
+        wqkv,
+        w_out,
+        ckv,
+        cosd,
+        sind,
+        cosd.T,
+        sind.T,
+        mask_t,
+        eye,
+        cache_keys,
+        cache_values,
+        first_moment,
+        second_moment,
+    )
+
+
 def solution(mesh):
     return jax.shard_map(
-        per_device,
+        fused_device if fits(mesh) else per_device,
         mesh=mesh,
         in_specs=(
             P(("groups", "dp"), "cache"),

time: 359 us -> 143 us (0.40)
  waiting for transfers between devices: 227 us -> 0 us
  Pallas kernels: 0 us -> 116 us
  blocking collectives: 66.9 us -> 0 us
  matrix products: 22.2 us -> 0 us
  between operations: 14.1 us -> 0.78 us
  local copies, waits for them, and re-layouts: 2.34 us -> 15.1 us
  starting transfers between devices: 9.15 us -> 0 us
  other arithmetic: 14.4 us -> 10.8 us
    all_gather x4 -> x0, waiting for transfers between devices: 210 us -> none  [the longest x1 86.4 us: per_device(): lax.all_gather(hidden, 'cache', axis=1, tiled=True)]
    pallas_call x0 -> x1, Pallas kernels: none -> 116 us  [fused_device(): pl.pallas_call(fused_kernel, out_shape=out_shape, in_specs=[vm, vm, vm, v...]
    all_gather x2 -> x0, blocking collectives: 66.9 us -> none  [the longest x1 35 us: per_device(): lax.all_gather(value_piece, 'cache', axis=2, tiled=True)]
    dot_general x10 -> x0, matrix products: 22.2 us -> none  [the longest x1 4.67 us: per_device(): lax.dot_general(grad_full, w_out, (((1,), (1,)), ((), ())), preferred_ele...]
    all_to_all x2 -> x0, waiting for transfers between devices: 15.3 us -> none  [the longest x1 7.64 us: per_device(): lax.all_to_all(send_k, ('cache', 'dp'), split_axis=0, concat_axis=0, tile...]
    all_to_all x2 -> x0, starting transfers between devices: 8.99 us -> none  [the longest x1 4.58 us: per_device(): lax.all_to_all(send_k, ('cache', 'dp'), split_axis=0, concat_axis=0, tile...]
    concatenate x0 -> x4, local copies, waits for them, and re-layouts: none -> 7.78 us  [the longest x2 6.21 us: fused_device(): jnp.concatenate([w_query, w_kv], axis=1)]
    unnamed x26 -> x14, local copies, waits for them, and re-layouts: 1.18 us -> 6.53 us
  transfers between devices with their start and end apart: 6 -> 0, of which waited for: 6 -> 0; matrix products, arithmetic and copies ran while one was open for 9% -> 0% of each run, Pallas kernels for 0% -> 0%
where the time goes in v1:
time: 143 us
  Pallas kernels  116 us (81%)
  local copies, waits for them, and re-layouts  15.1 us (11%)
  other arithmetic  10.8 us (8%)
    pallas_call x1, Pallas kernels, fused_device(): pl.pallas_call(fused_kernel, out_shape=out_shape, in_specs=[vm, vm, vm, v...  116 us
    unnamed x14, local copies, waits for them, and re-layouts  6.53 us
    concatenate x2, local copies, waits for them, and re-layouts, fused_device(): jnp.concatenate([w_query, w_kv], axis=1)  6.21 us
    concatenate x1, other arithmetic, fused_device(): jnp.concatenate([w_query, w_kv], axis=1)  4.16 us

profile of v1, /device:TPU:13, one launch (start us, length us, event | category | flops | bytes accessed | tf_op | source)
XLA Modules:
  0.0 142.5 jit_solution(12926003237147272262)
XLA Ops:
  0.6 1.1 multiply_reduce_fusion
  1.8 0.6 broadcast_in_dim.39.ss_in
  2.4 1.7 %pad_maximum_fusion.1 = bf16[8192,8,2,8]{0,3,1,2:T(8,128)(2,1)S(1)} fusion(bf16[8192,8,1,8]{0,3,1,2:T(8,128)(2,1)} %bitcast.33, bf16[8192,8,1,8]{0,3,1,2:T(8,128)(2,1)} %bitcast.34), kind=kLoop, calls=%fused_computation.1 | loop fusion | flops 1048576 | bytes 4194304 | tf_op jit(solution)/shard_map/stack | solution.py:639
  4.1 0.1 copy.28
  4.3 2.8 %concatenate.15 = bf16[4,4,512,128]{2,1,0,3:T(4,128)(2,1)} reshape(bf16[8192,8,2,8]{0,3,2,1:T(8,128)(2,1)S(1)} %copy.28) | data formatting | bytes 4194304 | tf_op jit(solution)/shard_map/concatenate | solution.py:640
  7.0 3.4 %copy.29 = bf16[4,4,512,128]{3,2,1,0:T(8,128)(2,1)S(1)} copy(bf16[4,4,512,128]{2,1,0,3:T(4,128)(2,1)} %concatenate.15) | data formatting | bytes 4194304 | tf_op jit(solution)/shard_map/concatenate | solution.py:640
  10.5 0.0 copy-start.3
  10.5 0.0 copy-start.2
  10.5 4.2 %pad_maximum_fusion.wqkv = bf16[4,4,512,256]{3,2,1,0:T(8,128)(2,1)} fusion(bf16[4,4,512,128]{3,2,1,0:T(8,128)(2,1)S(1)} %copy.29, bf16[4,4,512,128]{3,2,1,0:T(8,128)(2,1)} %bitcast.32), kind=kLoop, calls=%fused_computation | loop fusion | flops 8388608 | bytes 8388608 | tf_op jit(solution)/shard_map/concatenate | solution.py:640
  14.8 0.7 pad_maximum_fusion.4
  15.5 0.2 reduce-window.4
  15.7 0.1 convert_reduce_fusion
  15.8 0.1 select_reduce_fusion.1
  15.9 0.4 fusion.3
  16.3 0.8 fusion.4
  17.1 0.8 copy.32.cosd
  17.9 0.8 copy.33.sind
  18.7 0.9 fusion.1.mask_t
  19.6 0.6 fusion.2.eye
  20.2 115.8 %shard_map.156 = (f32[32,1024]{1,0:T(8,128)}, f32[32,1024]{1,0:T(8,128)}, f32[2,32,1024]{2,1,0:T(8,128)}, f32[2,32,1024]{2,1,0:T(8,128)}) custom-call(bf16[320,512]{1,0:T(8,128)(2,1)} %hid.1, bf16[320,512]{1,0:T(8,128)(2,1)} %og.1, f32[8,320]{1,0:T(8,128)} %broadcast_in_dim.39.ss_in, f32[16,1,512]{2,1,0:T(1,128)} %bitcast.38, ...), custom_call_target="tpu_custom_call" | custom-call | tf_op jit(solution)/shard_map/pallas_call | solution.py:662
  136.0 1.6 %copy.40 = f32[32,1024]{1,0:T(8,128)} copy(f32[32,1024]{1,0:T(8,128)} %get-tuple-element.19) | data formatting | bytes 262144
  137.6 1.6 %copy.41 = f32[32,1024]{1,0:T(8,128)} copy(f32[32,1024]{1,0:T(8,128)} %get-tuple-element.20) | data formatting | bytes 262144
  139.2 1.7 %copy.42 = f32[2,32,1024]{2,1,0:T(8,128)} copy(f32[2,32,1024]{2,1,0:T(8,128)} %get-tuple-element.21) | data formatting | bytes 524288
  140.9 1.7 %copy.43 = f32[2,32,1024]{2,1,0:T(8,128)} copy(f32[2,32,1024]{2,1,0:T(8,128)} %get-tuple-element.22) | data formatting | bytes 524288
  (15 shorter events, 0.1 us)
Async XLA Ops:
  10.5 4.2 %copy-start = (f32[32,1024]{1,0:T(8,128)S(1)}, f32[32,1024]{1,0:T(8,128)}, u32[]{:S(2)}) copy-start(f32[32,1024]{1,0:T(8,128)} %cv.1) | copy-start | bytes 393220
  10.5 4.3 %copy-start.1 = (f32[32,1024]{1,0:T(8,128)S(1)}, f32[32,1024]{1,0:T(8,128)}, u32[]{:S(2)}) copy-start(f32[32,1024]{1,0:T(8,128)} %ck.1) | copy-start | bytes 393220
  10.5 5.0 %copy-start.3 = (s32[1,4]{1,0:T(1,128)S(1)}, s32[1,4]{1,0:T(1,128)}, u32[]{:S(2)}) copy-start(s32[1,4]{1,0:T(1,128)} %param.24) | copy-start | bytes 52
  10.5 5.3 %copy-start.2 = (s32[1,4]{1,0:T(1,128)S(1)}, s32[1,4]{1,0:T(1,128)}, u32[]{:S(2)}) copy-start(s32[1,4]{1,0:T(1,128)} %param.25) | copy-start | bytes 52

commit v2 on v1

--- a/solution.py
+++ b/solution.py
@@ -216,29 +216,21 @@
 def fused_kernel(
     hid,
     og,
-    ss_in,
     gain,
-    wqkv,
+    wq,
+    wkv,
     wout,
     ckv,
     cosd,
     sind,
-    cos_t,
-    sin_t,
-    mask_t,
-    eye,
-    ck,
-    cv,
-    fm,
-    sm,
-    nk,
-    nv,
-    nf,
-    ns,
+    lengths,
+    total_grad,
     hbuf,
     obuf,
+    ss_in,
     srecv,
     wbuf,
+    wkbuf,
     wobuf,
     cbuf,
     cpart,
@@ -259,6 +251,10 @@
     w_r,
     wf_s,
     wf_r,
+    wk_s,
+    wk_r,
+    wkf_s,
+    wkf_r,
     wo_s,
     wo_r,
     wof_s,
@@ -299,7 +295,7 @@
 
     lax.fori_loop(1, devs, greet, 0)
 
-    own_w = pltpu.make_async_copy(wqkv.at[:, p], wbuf.at[0], loc.at[0])
+    own_w = pltpu.make_async_copy(wq.at[:, p], wbuf.at[0], loc.at[0])
     own_w.start()
     own_wo = []
     for zz in range(LINE):
@@ -307,8 +303,21 @@
         cp = pltpu.make_async_copy(wout.at[:, pl.ds(col, width)], wobuf.at[0, zz], loco.at[zz])
         cp.start()
         own_wo.append(cp)
+        cp = pltpu.make_async_copy(
+            wkv.at[:, pl.ds(col, width)], wkbuf.at[0, zz], loco.at[LINE + zz]
+        )
+        cp.start()
+        own_wo.append(cp)
     own_c = pltpu.make_async_copy(ckv.at[m // (chips // KV)], cbuf.at[i], loc.at[1])
     own_c.start()
+    own_f = hid[...].astype(f32)
+    ss_in[...] = lax.dot_general(
+        jnp.ones((8, width), f32),
+        own_f * own_f,
+        (((1,), (1,)), ((), ())),
+        preferred_element_type=f32,
+        precision=lax.Precision.HIGHEST,
+    )
     pl.semaphore_wait(barrier, devs - 1)
 
     def remote(src, dst, ss, rs, chip, core):
@@ -339,28 +348,53 @@
     def back_chip(k):
         return line * PLANE + (p + PLANE - k) % PLANE
 
-    o_cp, h_cp, w_cp, wo_cp = {}, {}, {}, {}
-    for k in range(1, LINE):
+    inner = jnp.logical_and(line > 0, line < LINE - 1)
+
+    def direct(k):
+        if k == LINE - 1:
+            return line != 0
+        if k == 1:
+            return line != LINE - 1
+        return None
+
+    def when(cond, act):
+        if cond is None:
+            act()
+        else:
+            pl.when(cond)(act)
+
+    def relay(buf, ss, rs):
+        slot = 2 * line - 1
+        return remote(
+            buf.at[2], buf.at[slot], ss.at[0], rs.at[slot], 3 * (line - 1) * PLANE + p, c
+        )
+
+    o_cp, h_cp, w_cp, wo_cp, wk_cp = {}, {}, {}, {}, {}
+    for k in (2, 1, 3):
         o_cp[k] = remote(og, obuf.at[k], o_s.at[k], o_r.at[k], line_chip(k), c)
-        o_cp[k].start()
-    for k in range(1, PLANE):
-        for h in range(pair):
-            col = pl.multiple_of(((mine + h) * PLANE + (p + k) % PLANE) * width, width)
-            wo_cp[k, h] = remote(
-                wout.at[:, pl.ds(col, width)],
-                wobuf.at[k, mine + h],
-                wo_s.at[k, h],
-                wo_r.at[k, h],
-                plane_chip(k),
-                c,
-            )
-            wo_cp[k, h].start()
-    for k in range(1, LINE):
+        when(direct(k), o_cp[k].start)
+
+    def send_rows(src, buf, ss, rs, cps):
+        for k in range(1, PLANE):
+            for h in range(pair):
+                col = pl.multiple_of(((mine + h) * PLANE + (p + k) % PLANE) * width, width)
+                cps[k, h] = remote(
+                    src.at[:, pl.ds(col, width)],
+                    buf.at[k, mine + h],
+                    ss.at[k, h],
+                    rs.at[k, h],
+                    plane_chip(k),
+                    c,
+                )
+                cps[k, h].start()
+
+    send_rows(wout, wobuf, wo_s, wo_r, wo_cp)
+    for k in (2, 1, 3):
         h_cp[k] = remote(hid, hbuf.at[k], h_s.at[k], h_r.at[k], line_chip(k), c)
-        h_cp[k].start()
+        when(direct(k), h_cp[k].start)
     for k in range(1, PLANE):
         w_cp[k] = remote(
-            wqkv.at[pl.ds(mine, pair), (p + k) % PLANE],
+            wq.at[pl.ds(mine, pair), (p + k) % PLANE],
             wbuf.at[k, pl.ds(mine, pair)],
             w_s.at[k],
             w_r.at[k],
@@ -368,6 +402,7 @@
             c,
         )
         w_cp[k].start()
+    send_rows(wkv, wkbuf, wk_s, wk_r, wk_cp)
 
     def c_copy(k):
         j = (i + k) % devs
@@ -380,6 +415,12 @@
         return carry
 
     lax.fori_loop(1, devs, start_c, 0)
+
+    o_cp[2].wait_recv()
+
+    @pl.when(inner)
+    def _():
+        relay(obuf, o_s, o_r).start()
 
     wof_cp = {}
     for k in range(1, PLANE):
@@ -404,7 +445,8 @@
         if kz == 0:
             block = og[...]
         else:
-            o_cp[kz].wait_recv()
+            if kz != 2:
+                o_cp[kz].wait_recv()
             block = obuf[kz]
         zz = (line + LINE - kz) % LINE
 
@@ -425,12 +467,40 @@
         rd_cp[k] = remote(dpart.at[k], drecv.at[k], rd_s.at[k], rd_r.at[k], back_chip(k), c)
         rd_cp[k].start()
 
-    wf_cp = {}
+    h_cp[2].wait_recv()
+
+    @pl.when(inner)
+    def _():
+        relay(hbuf, h_s, h_r).start()
+
+    wf_cp, wkf_cp = {}, {}
     for k in range(1, PLANE):
         w_cp[k].wait_recv()
         part = wbuf.at[k, pl.ds(mine, pair)]
         wf_cp[k] = remote(part, part, wf_s.at[k], wf_r.at[k], m, 1 - c)
         wf_cp[k].start()
+        for h in range(pair):
+            wk_cp[k, h].wait_recv()
+            part = wkbuf.at[k, mine + h]
+            wkf_cp[k, h] = remote(part, part, wkf_s.at[k, h], wkf_r.at[k, h], m, 1 - c)
+            wkf_cp[k, h].start()
+
+    unit = (
+        lax.broadcasted_iota(jnp.int32, (128, 128), 0)
+        == lax.broadcasted_iota(jnp.int32, (128, 128), 1)
+    ).astype(f32)
+    eye = unit.astype(bf16)
+
+    def flip(table):
+        return lax.dot_general(
+            unit,
+            table,
+            (((1,), (1,)), ((), ())),
+            preferred_element_type=f32,
+            precision=lax.Precision.HIGHEST,
+        )
+
+    cos_t, sin_t = flip(cosd[...]), flip(sind[...])
 
     def wait_ss(k, carry):
         ss_copy(k).wait()
@@ -450,21 +520,29 @@
     own_w.wait()
     for k in range(1, PLANE):
         wf_cp[k].wait_recv()
+        for h in range(pair):
+            wkf_cp[k, h].wait_recv()
     for kz in range(LINE):
         zz = (line + LINE - kz) % LINE
         if kz == 0:
             block = hid[...]
         else:
-            h_cp[kz].wait_recv()
+            if kz != 2:
+                h_cp[kz].wait_recv()
             block = hbuf[kz]
         normed = (block.astype(f32) * inv * gain[zz * PLANE + p]).astype(bf16)
 
         def add_c(k, carry):
             term = jnp.dot(normed, wbuf[k, zz], preferred_element_type=f32)
+            term_kv = lax.dot_general(
+                normed, wkbuf[k, zz], (((1,), (1,)), ((), ())), preferred_element_type=f32
+            )
             if kz == 0:
-                cpart[k] = term
+                cpart[k, :, :128] = term
+                cpart[k, :, 128:] = term_kv
             else:
-                cpart[k] = cpart[k] + term
+                cpart[k, :, :128] = cpart[k, :, :128] + term
+                cpart[k, :, 128:] = cpart[k, :, 128:] + term_kv
             return carry
 
         lax.fori_loop(0, PLANE, add_c, 0)
@@ -480,7 +558,7 @@
         grad = grad + drecv[k]
     grad = grad.astype(bf16)
     grad_t = lax.dot_general(
-        eye[...], grad, (((1,), (1,)), ((), ())), preferred_element_type=f32
+        eye, grad, (((1,), (1,)), ((), ())), preferred_element_type=f32
     )
     own_c.wait()
 
@@ -489,7 +567,7 @@
         return carry
 
     lax.fori_loop(1, devs, wait_c, 0)
-    rows = ck.shape[0]
+    rows = total_grad.shape[1]
     cache_len = rows * devs
     head_k = cbuf[:, :rows, :].reshape(cache_len, 128)
     head_v = cbuf[:, rows:, :].reshape(cache_len, 128)
@@ -503,7 +581,7 @@
         qkv = qkv + crecv[k]
     kv = qkv[:, 128:].astype(bf16)
     kvt[...] = lax.dot_general(
-        eye[...], kv, (((1,), (1,)), ((), ())), preferred_element_type=f32
+        eye, kv, (((1,), (1,)), ((), ())), preferred_element_type=f32
     ).astype(bf16)
 
     def kv_part(chip):
@@ -526,7 +604,7 @@
     turned = jnp.concatenate([q_raw[:, 64:], q_raw[:, :64]], axis=1)
     query = (q_raw * cosd[...] + turned * sind[...]).astype(bf16)
     query_t = lax.dot_general(
-        eye[...], query, (((1,), (1,)), ((), ())), preferred_element_type=f32
+        eye, query, (((1,), (1,)), ((), ())), preferred_element_type=f32
     ).astype(bf16)
     score = jnp.dot(head_k, query_t, preferred_element_type=f32) * scale
     top = jnp.max(score, axis=0, keepdims=True)
@@ -541,12 +619,19 @@
     key_t = kvf[:, :8, :].reshape(128, kvf.shape[2])
     value_t = kvf[:, 8:, :].reshape(128, kvf.shape[2]).astype(bf16)
     turned_t = jnp.concatenate([key_t[64:], key_t[:64]], axis=0)
-    key_t = (key_t * cos_t[...] + turned_t * sin_t[...]).astype(bf16)
+    key_t = (key_t * cos_t + turned_t * sin_t).astype(bf16)
     score_self = (
         lax.dot_general(key_t, query_t, (((0,), (0,)), ((), ())), preferred_element_type=f32)
         * scale
     )
-    score_self = jnp.where(mask_t[...] > 0.5, score_self, -1e30)
+    source = lax.broadcasted_iota(jnp.int32, score_self.shape, 0)
+    target = lax.broadcasted_iota(jnp.int32, score_self.shape, 1)
+    first, last = jnp.zeros_like(target), lengths[0, 0]
+    for n in range(1, lengths.shape[1]):
+        first = jnp.where(target >= last, last, first)
+        last = last + lengths[0, n]
+    allowed = jnp.logical_and(source <= target, source >= first)
+    score_self = jnp.where(allowed, score_self, -1e30)
     top = jnp.maximum(top, jnp.max(score_self, axis=0, keepdims=True))
     e_cache = jnp.exp(score - top)
     e_self = jnp.exp(score_self - top)
@@ -579,8 +664,14 @@
     own_g.start()
 
     for k in range(1, LINE):
-        o_cp[k].wait_send()
-        h_cp[k].wait_send()
+        when(direct(k), o_cp[k].wait_send)
+        when(direct(k), h_cp[k].wait_send)
+
+    @pl.when(inner)
+    def _():
+        relay(obuf, o_s, o_r).wait_send()
+        relay(hbuf, h_s, h_r).wait_send()
+
     for k in range(1, PLANE):
         w_cp[k].wait_send()
         wf_cp[k].wait_send()
@@ -589,6 +680,8 @@
         for h in range(pair):
             wo_cp[k, h].wait_send()
             wof_cp[k, h].wait_send()
+            wk_cp[k, h].wait_send()
+            wkf_cp[k, h].wait_send()
 
     def wait_g(k, carry):
         g_copy(k).wait()
@@ -601,14 +694,8 @@
     for g in range(KV):
         got = jnp.sum(grecv[g * share : (g + 1) * share].astype(f32), axis=0)
         cols = slice(g * 128, (g + 1) * 128)
-        for which, master, out in ((0, ck, nk), (1, cv, nv)):
-            gradient = got[which * rows : (which + 1) * rows]
-            new, first, second = adam_update(
-                master[:, cols], gradient, fm[which, :, cols], sm[which, :, cols]
-            )
-            out[:, cols] = new
-            nf[which, :, cols] = first
-            ns[which, :, cols] = second
+        for which in range(2):
+            total_grad[which, :, cols] = got[which * rows : (which + 1) * rows]
 
 
 def fused_device(
@@ -634,10 +721,8 @@
     cache_len = pos * devs
     head = w_query.shape[1]
     full = w_query.shape[0]
-    hf = hidden.astype(f32)
-    squares = jnp.broadcast_to(jnp.sum(hf * hf, axis=1)[None, :], (8, rows))
-    w_kv = jnp.stack([w_key, w_value], axis=2).reshape(full, head)
-    wqkv = jnp.concatenate([w_query, w_kv], axis=1).reshape(LINE, PLANE, width, 2 * head)
+    w_kv = jnp.stack([w_key.transpose(1, 2, 0), w_value.transpose(1, 2, 0)], axis=1)
+    w_kv = w_kv.reshape(head, full)
     ckv = jnp.stack(
         [cache_keys.astype(bf16).reshape(pos, KV, head), cache_values.astype(bf16).reshape(pos, KV, head)]
     )
@@ -646,29 +731,23 @@
     cos, sin = rope_tables(position, head)
     cosd = jnp.concatenate([cos, cos], axis=1)
     sind = jnp.concatenate([-sin, sin], axis=1)
-    index = jnp.arange(rows, dtype=jnp.int32)
-    mask_t = ((segment[:, None] == segment[None, :]) & (index[:, None] <= index[None, :])).astype(f32)
-    eye = jnp.eye(head, dtype=bf16)
     vm = pl.BlockSpec(memory_space=pltpu.VMEM)
+    smem = pl.BlockSpec(memory_space=pltpu.SMEM)
     hbm = pl.BlockSpec(memory_space=pl.ANY)
     dma = pltpu.SemaphoreType.DMA
     pair = LINE // 2
-    out_shape = (
-        jax.ShapeDtypeStruct(cache_keys.shape, f32),
-        jax.ShapeDtypeStruct(cache_keys.shape, f32),
-        jax.ShapeDtypeStruct(first_moment.shape, f32),
-        jax.ShapeDtypeStruct(first_moment.shape, f32),
-    )
-    return pl.pallas_call(
+    gradient = pl.pallas_call(
         fused_kernel,
-        out_shape=out_shape,
-        in_specs=[vm, vm, vm, vm, hbm, hbm] + [vm] * 11,
-        out_specs=(vm,) * 4,
+        out_shape=jax.ShapeDtypeStruct(first_moment.shape, f32),
+        in_specs=[vm, vm, vm, hbm, hbm, hbm, vm, vm, vm, smem],
+        out_specs=vm,
         scratch_shapes=[
             pltpu.VMEM((LINE, rows, width), bf16),
             pltpu.VMEM((LINE, rows, width), bf16),
+            pltpu.VMEM((8, rows), f32),
             pltpu.VMEM((chips, 8, rows), f32),
-            pltpu.VMEM((PLANE, LINE, width, 2 * head), bf16),
+            pltpu.VMEM((PLANE, LINE, width, head), bf16),
+            pltpu.VMEM((PLANE, LINE, head, width), bf16),
             pltpu.VMEM((PLANE, LINE, head, width), bf16),
             pltpu.VMEM((devs, 2 * pos, head), bf16),
             pltpu.VMEM((PLANE, rows, 2 * head), f32),
@@ -693,6 +772,10 @@
             dma((PLANE, pair)),
             dma((PLANE, pair)),
             dma((PLANE, pair)),
+            dma((PLANE, pair)),
+            dma((PLANE, pair)),
+            dma((PLANE, pair)),
+            dma((PLANE, pair)),
             dma((devs,)),
             dma((devs,)),
             dma((PLANE,)),
@@ -704,7 +787,7 @@
             dma((devs,)),
             dma((devs,)),
             dma((4,)),
-            dma((LINE,)),
+            dma((2 * LINE,)),
         ],
         compiler_params=pltpu.CompilerParams(
             collective_id=0, has_side_effects=True, vmem_limit_bytes=56 * 1024 * 1024
@@ -712,22 +795,22 @@
     )(
         hidden,
         out_grad,
-        squares,
         norm_gain.reshape(chips, 1, width),
-        wqkv,
+        w_query.reshape(LINE, PLANE, width, head),
+        w_kv,
         w_out,
         ckv,
         cosd,
         sind,
-        cosd.T,
-        sind.T,
-        mask_t,
-        eye,
-        cache_keys,
-        cache_values,
-        first_moment,
-        second_moment,
-    )
+        conv_lengths,
+    )
+    new_keys, first_k, second_k = adam_update(
+        cache_keys, gradient[0], first_moment[0], second_moment[0]
+    )
+    new_values, first_v, second_v = adam_update(
+        cache_values, gradient[1], first_moment[1], second_moment[1]
+    )
+    return (new_keys, new_values, jnp.stack([first_k, first_v]), jnp.stack([second_k, second_v]))
 
 
 def solution(mesh):

time: 143 us -> 115 us (0.80)
  local copies, waits for them, and re-layouts: 15.1 us -> 1.58 us
  Pallas kernels: 116 us -> 104 us
  other arithmetic: 10.8 us -> 8.67 us
    pallas_call x1, Pallas kernels: 116 us -> 104 us  [fused_device(): pl.pallas_call(fused_kernel, out_shape=jax.ShapeDtypeStruct(first_moment....]
    concatenate x4 -> x0, local copies, waits for them, and re-layouts: 7.78 us -> none  [the longest x2 6.21 us: fused_device(): jnp.concatenate([w_query, w_kv], axis=1)]
    unnamed x14, local copies, waits for them, and re-layouts: 6.53 us -> 0.06 us
    concatenate x1, other arithmetic: 4.16 us -> 0.88 us  [fused_device(): cosd = jnp.concatenate([cos, cos], axis=1)]
    sub x0 -> x1, other arithmetic: none -> 1.85 us  [adam_update(): master - RATE * first_hat / (jnp.sqrt(second_hat) + EPSILON)]
    convert_element_type x2 -> x0, other arithmetic: 1.51 us -> none  [the longest x1 0.88 us: fused_device(): ((segment[:, None] == segment[None, :]) & (index[:, None] <= index[None,...]
    another operation x2 -> x4, other arithmetic: 1.91 us -> 3.35 us  [the longest x1 1.73 us: fused_device(): jnp.stack([w_key.transpose(1, 2, 0), w_value.transpose(1, 2, 0)], axis=1)]
where the time goes in v2:
time: 115 us
  Pallas kernels  104 us (90%)
  other arithmetic  8.67 us (8%)
  local copies, waits for them, and re-layouts  1.58 us (1%)
    pallas_call x1, Pallas kernels, fused_device(): pl.pallas_call(fused_kernel, out_shape=jax.ShapeDtypeStruct(first_moment....  104 us

profile of v2, /device:TPU:13, one launch (start us, length us, event | category | flops | bytes accessed | tf_op | source)
XLA Modules:
  0.0 114.8 jit_solution(5910537294422720556)
XLA Ops:
  0.6 1.7 %pad_maximum_fusion = bf16[8,2,8,8192]{3,2,0,1:T(8,128)(2,1)S(1)} fusion(bf16[8,1,8,8192]{3,2,0,1:T(8,128)(2,1)} %bitcast.57, bf16[8,1,8,8192]{3,2,0,1:T(8,128)(2,1)} %bitcast.58), kind=kLoop, calls=%fused_computation | loop fusion | flops 1048576 | bytes 4194304 | tf_op jit(solution)/shard_map/stack | solution.py:724
  2.4 0.0 copy-start.2
  2.4 0.0 copy-start.3
  2.4 0.0 copy-start.4
  2.4 0.0 copy-start.5
  2.4 1.5 %copy.20 = bf16[8,2,8,8192]{3,2,1,0:T(8,128)(2,1)} copy(bf16[8,2,8,8192]{3,2,0,1:T(8,128)(2,1)S(1)} %pad_maximum_fusion) | data formatting | bytes 4194304 | tf_op jit(solution)/shard_map/stack | solution.py:724
  3.9 0.0 copy-done.2
  4.0 0.0 copy-done.3
  4.0 0.7 pad_maximum_fusion.5
  4.7 0.0 copy-done.4
  4.7 0.2 reduce-window.4
  4.9 0.1 convert_reduce_fusion
  5.0 0.0 copy-done.5
  5.0 0.1 select_reduce_fusion.1
  5.1 0.6 fusion.18
  5.8 0.9 pad_maximum_fusion.3
  6.6 0.0 copy-start
  6.7 103.8 %shard_map.156 = f32[2,32,1024]{2,1,0:T(8,128)} custom-call(bf16[320,512]{1,0:T(8,128)(2,1)} %hid.1, bf16[320,512]{1,0:T(8,128)(2,1)} %og.1, f32[16,1,512]{2,1,0:T(1,128)} %bitcast.62, bf16[4,4,512,128]{3,2,1,0:T(8,128)(2,1)} %bitcast.56, bf16[128,8192]{1,0:T(8,128)(2,1)} %bitcast.55, bf16[128,8192]{1,0:T(8,128)(2,1)} %wout.1, bf16[8,64,128]{2,1,0:T(8,128)(2,1)} %bitcast.59, ...), custom_call_target="tpu_custom_call" | custom-call | tf_op jit(solution)/shard_map/pallas_call | solution.py:739
  110.4 0.0 copy-done
  110.4 0.0 copy-done.1
  110.5 1.8 %fusion.11 = (f32[32,1024]{1,0:T(8,128)}, f32[32,1024]{1,0:T(8,128)}) fusion(f32[32,1024]{1,0:T(8,128)S(1)} %copy-done.2, f32[2,32,1024]{2,1,0:T(8,128)S(1)} %copy-done, f32[2,32,1024]{2,1,0:T(8,128)S(1)} %copy-done.1, f32[2,32,1024]{2,1,0:T(8,128)} %shard_map.156, f32[32,1024]{1,0:T(8,128)S(1)} %copy-done.3), kind=kLoop, calls=%fused_computation.22 | loop fusion | flops 786432 | bytes 1310720 | tf_op jit(solution)/shard_map/sub | solution.py:89
  112.3 1.0 fusion.12
  113.4 0.7 pad_maximum_fusion.1
  114.1 0.7 pad_maximum_fusion.2
  (10 shorter events, 0.1 us)
Async XLA Ops:
  2.4 1.5 %copy-start.2 = (f32[32,1024]{1,0:T(8,128)S(1)}, f32[32,1024]{1,0:T(8,128)}, u32[]{:S(2)}) copy-start(f32[32,1024]{1,0:T(8,128)} %param.21) | copy-start | bytes 393220
  2.4 1.6 %copy-start.3 = (f32[32,1024]{1,0:T(8,128)S(1)}, f32[32,1024]{1,0:T(8,128)}, u32[]{:S(2)}) copy-start(f32[32,1024]{1,0:T(8,128)} %param.20) | copy-start | bytes 393220
  2.4 2.3 %copy-start.4 = (s32[1,4]{1,0:T(1,128)S(1)}, s32[1,4]{1,0:T(1,128)}, u32[]{:S(2)}) copy-start(s32[1,4]{1,0:T(1,128)} %lengths.1) | copy-start | bytes 52
  2.4 2.6 %copy-start.5 = (s32[1,4]{1,0:T(1,128)S(1)}, s32[1,4]{1,0:T(1,128)}, u32[]{:S(2)}) copy-start(s32[1,4]{1,0:T(1,128)} %param.25) | copy-start | bytes 52
  6.6 103.8 %copy-start = (f32[2,32,1024]{2,1,0:T(8,128)S(1)}, f32[2,32,1024]{2,1,0:T(8,128)}, u32[]{:S(2)}) copy-start(f32[2,32,1024]{2,1,0:T(8,128)} %param.22) | copy-start | bytes 786436
  6.7 103.8 %copy-start.1 = (f32[2,32,1024]{2,1,0:T(8,128)S(1)}, f32[2,32,1024]{2,1,0:T(8,128)}, u32[]{:S(2)}) copy-start(f32[2,32,1024]{2,1,0:T(8,128)} %param.23) | copy-start | bytes 786436

commit v3 on v2

--- a/solution.py
+++ b/solution.py
@@ -435,6 +435,12 @@
                 1 - c,
             )
             wof_cp[k, h].start()
+
+    @pl.when(inner)
+    def _():
+        h_cp[2].wait_recv()
+        relay(hbuf, h_s, h_r).start()
+
     for cp in own_wo:
         cp.wait()
     for k in range(1, PLANE):
@@ -467,12 +473,7 @@
         rd_cp[k] = remote(dpart.at[k], drecv.at[k], rd_s.at[k], rd_r.at[k], back_chip(k), c)
         rd_cp[k].start()
 
-    h_cp[2].wait_recv()
-
-    @pl.when(inner)
-    def _():
-        relay(hbuf, h_s, h_r).start()
-
+    pl.when(jnp.logical_not(inner))(h_cp[2].wait_recv)
     wf_cp, wkf_cp = {}, {}
     for k in range(1, PLANE):
         w_cp[k].wait_recv()
@@ -641,25 +642,32 @@
     prob = e_cache * inverse
     weight = prob.astype(bf16)
     weight_self = (e_self * inverse).astype(bf16)
+    value_part = jnp.dot(weight, grad, preferred_element_type=f32).astype(bf16)
+    gsend[:, rows:, :] = value_part.reshape(devs, rows, 128)
+
+    def g_copy(k, which):
+        j = (i + k) % devs
+        part = pl.ds(which * rows, rows)
+        return remote(
+            gsend.at[j, part], grecv.at[i, part], g_s.at[which, k], g_r.at[which, k], j // 2, j % 2
+        )
+
+    def start_g(which):
+        def start(k, carry):
+            g_copy(k, which).start()
+            return carry
+
+        lax.fori_loop(1, devs, start, 0)
+
+    start_g(1)
     attended = lax.dot_general(
         head_v, weight, (((0,), (0,)), ((), ())), preferred_element_type=f32
     ) + jnp.dot(value_t, weight_self, preferred_element_type=f32)
     delta = jnp.sum(grad_t * attended, axis=0, keepdims=True)
     grad_score = (prob * (grad_prob - delta)).astype(bf16)
-    value_part = jnp.dot(weight, grad, preferred_element_type=f32).astype(bf16)
     key_part = (jnp.dot(grad_score, query, preferred_element_type=f32) * scale).astype(bf16)
     gsend[:, :rows, :] = key_part.reshape(devs, rows, 128)
-    gsend[:, rows:, :] = value_part.reshape(devs, rows, 128)
-
-    def g_copy(k):
-        j = (i + k) % devs
-        return remote(gsend.at[j], grecv.at[i], g_s.at[k], g_r.at[k], j // 2, j % 2)
-
-    def start_g(k, carry):
-        g_copy(k).start()
-        return carry
-
-    lax.fori_loop(1, devs, start_g, 0)
+    start_g(0)
     own_g = pltpu.make_async_copy(gsend.at[i], grecv.at[i], loc.at[3])
     own_g.start()
 
@@ -684,7 +692,8 @@
             wkf_cp[k, h].wait_send()
 
     def wait_g(k, carry):
-        g_copy(k).wait()
+        g_copy(k, 1).wait()
+        g_copy(k, 0).wait()
         return carry
 
     lax.fori_loop(1, devs, wait_g, 0)
@@ -784,8 +793,8 @@
             dma((PLANE,)),
             dma((chips,)),
             dma((chips,)),
-            dma((devs,)),
-            dma((devs,)),
+            dma((2, devs)),
+            dma((2, devs)),
             dma((4,)),
             dma((2 * LINE,)),
         ],

time: 115 us -> 116 us (level); the launches traced: 115 us -> 114 us
  no operation moved by 1% of the time
where the time goes in v3:
time: 116 us; the launch traced here: 114 us
  Pallas kernels  103 us (89%)
  other arithmetic  8.67 us (7%)
  local copies, waits for them, and re-layouts  1.58 us (1%)
    pallas_call x1, Pallas kernels, fused_device(): pl.pallas_call(fused_kernel, out_shape=jax.ShapeDtypeStruct(first_moment....  103 us

profile of v3, /device:TPU:13, one launch (start us, length us, event | category | flops | bytes accessed | tf_op | source)
XLA Modules:
  0.0 114.0 jit_solution(6759746628959464195)
XLA Ops:
  0.6 1.7 %pad_maximum_fusion = bf16[8,2,8,8192]{3,2,0,1:T(8,128)(2,1)S(1)} fusion(bf16[8,1,8,8192]{3,2,0,1:T(8,128)(2,1)} %bitcast.57, bf16[8,1,8,8192]{3,2,0,1:T(8,128)(2,1)} %bitcast.58), kind=kLoop, calls=%fused_computation | loop fusion | flops 1048576 | bytes 4194304 | tf_op jit(solution)/shard_map/stack | solution.py:733
  2.4 0.0 copy-start.2
  2.4 0.0 copy-start.3
  2.4 0.0 copy-start.4
  2.4 0.0 copy-start.5
  2.4 1.5 %copy.20 = bf16[8,2,8,8192]{3,2,1,0:T(8,128)(2,1)} copy(bf16[8,2,8,8192]{3,2,0,1:T(8,128)(2,1)S(1)} %pad_maximum_fusion) | data formatting | bytes 4194304 | tf_op jit(solution)/shard_map/stack | solution.py:733
  3.9 0.0 copy-done.2
  4.0 0.0 copy-done.3
  4.0 0.7 pad_maximum_fusion.5
  4.7 0.0 copy-done.4
  4.7 0.2 reduce-window.4
  4.9 0.1 convert_reduce_fusion
  5.0 0.0 copy-done.5
  5.0 0.1 select_reduce_fusion.1
  5.1 0.6 fusion.18
  5.8 0.9 pad_maximum_fusion.3
  6.6 0.0 copy-start
  6.7 102.9 %shard_map.156 = f32[2,32,1024]{2,1,0:T(8,128)} custom-call(bf16[320,512]{1,0:T(8,128)(2,1)} %hid.1, bf16[320,512]{1,0:T(8,128)(2,1)} %og.1, f32[16,1,512]{2,1,0:T(1,128)} %bitcast.62, bf16[4,4,512,128]{3,2,1,0:T(8,128)(2,1)} %bitcast.56, bf16[128,8192]{1,0:T(8,128)(2,1)} %bitcast.55, bf16[128,8192]{1,0:T(8,128)(2,1)} %wout.1, bf16[8,64,128]{2,1,0:T(8,128)(2,1)} %bitcast.59, ...), custom_call_target="tpu_custom_call" | custom-call | tf_op jit(solution)/shard_map/pallas_call | solution.py:748
  109.6 0.0 copy-done
  109.6 0.0 copy-done.1
  109.6 1.8 %fusion.11 = (f32[32,1024]{1,0:T(8,128)}, f32[32,1024]{1,0:T(8,128)}) fusion(f32[32,1024]{1,0:T(8,128)S(1)} %copy-done.2, f32[2,32,1024]{2,1,0:T(8,128)S(1)} %copy-done, f32[2,32,1024]{2,1,0:T(8,128)S(1)} %copy-done.1, f32[2,32,1024]{2,1,0:T(8,128)} %shard_map.156, f32[32,1024]{1,0:T(8,128)S(1)} %copy-done.3), kind=kLoop, calls=%fused_computation.22 | loop fusion | flops 786432 | bytes 1310720 | tf_op jit(solution)/shard_map/sub | solution.py:89
  111.5 1.0 fusion.12
  112.5 0.7 pad_maximum_fusion.1
  113.2 0.7 pad_maximum_fusion.2
  (10 shorter events, 0.1 us)
Async XLA Ops:
  2.4 1.5 %copy-start.2 = (f32[32,1024]{1,0:T(8,128)S(1)}, f32[32,1024]{1,0:T(8,128)}, u32[]{:S(2)}) copy-start(f32[32,1024]{1,0:T(8,128)} %param.21) | copy-start | bytes 393220
  2.4 1.6 %copy-start.3 = (f32[32,1024]{1,0:T(8,128)S(1)}, f32[32,1024]{1,0:T(8,128)}, u32[]{:S(2)}) copy-start(f32[32,1024]{1,0:T(8,128)} %param.20) | copy-start | bytes 393220
  2.4 2.3 %copy-start.4 = (s32[1,4]{1,0:T(1,128)S(1)}, s32[1,4]{1,0:T(1,128)}, u32[]{:S(2)}) copy-start(s32[1,4]{1,0:T(1,128)} %lengths.1) | copy-start | bytes 52
  2.4 2.6 %copy-start.5 = (s32[1,4]{1,0:T(1,128)S(1)}, s32[1,4]{1,0:T(1,128)}, u32[]{:S(2)}) copy-start(s32[1,4]{1,0:T(1,128)} %param.25) | copy-start | bytes 52
  6.6 103.0 %copy-start = (f32[2,32,1024]{2,1,0:T(8,128)S(1)}, f32[2,32,1024]{2,1,0:T(8,128)}, u32[]{:S(2)}) copy-start(f32[2,32,1024]{2,1,0:T(8,128)} %param.22) | copy-start | bytes 786436
  6.7 103.0 %copy-start.1 = (f32[2,32,1024]{2,1,0:T(8,128)S(1)}, f32[2,32,1024]{2,1,0:T(8,128)}, u32[]{:S(2)}) copy-start(f32[2,32,1024]{2,1,0:T(8,128)} %param.23) | copy-start | bytes 786436

commit v4 on v2

--- a/solution.py
+++ b/solution.py
@@ -370,10 +370,6 @@
         )
 
     o_cp, h_cp, w_cp, wo_cp, wk_cp = {}, {}, {}, {}, {}
-    for k in (2, 1, 3):
-        o_cp[k] = remote(og, obuf.at[k], o_s.at[k], o_r.at[k], line_chip(k), c)
-        when(direct(k), o_cp[k].start)
-
     def send_rows(src, buf, ss, rs, cps):
         for k in range(1, PLANE):
             for h in range(pair):
@@ -388,7 +384,6 @@
                 )
                 cps[k, h].start()
 
-    send_rows(wout, wobuf, wo_s, wo_r, wo_cp)
     for k in (2, 1, 3):
         h_cp[k] = remote(hid, hbuf.at[k], h_s.at[k], h_r.at[k], line_chip(k), c)
         when(direct(k), h_cp[k].start)
@@ -416,57 +411,11 @@
 
     lax.fori_loop(1, devs, start_c, 0)
 
-    o_cp[2].wait_recv()
-
-    @pl.when(inner)
-    def _():
-        relay(obuf, o_s, o_r).start()
-
-    wof_cp = {}
-    for k in range(1, PLANE):
-        for h in range(pair):
-            wo_cp[k, h].wait_recv()
-            wof_cp[k, h] = remote(
-                wobuf.at[k, mine + h],
-                wobuf.at[k, mine + h],
-                wof_s.at[k, h],
-                wof_r.at[k, h],
-                m,
-                1 - c,
-            )
-            wof_cp[k, h].start()
-    for cp in own_wo:
-        cp.wait()
-    for k in range(1, PLANE):
-        for h in range(pair):
-            wof_cp[k, h].wait_recv()
-
-    for kz in range(LINE):
-        if kz == 0:
-            block = og[...]
-        else:
-            if kz != 2:
-                o_cp[kz].wait_recv()
-            block = obuf[kz]
-        zz = (line + LINE - kz) % LINE
-
-        def add_d(k, carry):
-            term = lax.dot_general(
-                block, wobuf[k, zz], (((1,), (1,)), ((), ())), preferred_element_type=f32
-            )
-            if kz == 0:
-                dpart[k] = term
-            else:
-                dpart[k] = dpart[k] + term
-            return carry
-
-        lax.fori_loop(0, PLANE, add_d, 0)
-
-    rd_cp = {}
-    for k in range(1, PLANE):
-        rd_cp[k] = remote(dpart.at[k], drecv.at[k], rd_s.at[k], rd_r.at[k], back_chip(k), c)
-        rd_cp[k].start()
-
+    for k in (2, 1, 3):
+        o_cp[k] = remote(og, obuf.at[k], o_s.at[k], o_r.at[k], line_chip(k), c)
+        when(direct(k), o_cp[k].start)
+
+    send_rows(wout, wobuf, wo_s, wo_r, wo_cp)
     h_cp[2].wait_recv()
 
     @pl.when(inner)
@@ -518,6 +467,8 @@
     )
     inv = lax.rsqrt(spread[:, :1] * (1.0 / (width * chips)) + 1e-05)
     own_w.wait()
+    for cp in own_wo:
+        cp.wait()
     for k in range(1, PLANE):
         wf_cp[k].wait_recv()
         for h in range(pair):
@@ -552,29 +503,25 @@
         rc_cp[k] = remote(cpart.at[k], crecv.at[k], rc_s.at[k], rc_r.at[k], back_chip(k), c)
         rc_cp[k].start()
 
-    grad = dpart[0]
-    for k in range(1, PLANE):
-        rd_cp[k].wait_recv()
-        grad = grad + drecv[k]
-    grad = grad.astype(bf16)
-    grad_t = lax.dot_general(
-        eye, grad, (((1,), (1,)), ((), ())), preferred_element_type=f32
-    )
-    own_c.wait()
-
-    def wait_c(k, carry):
-        c_copy(k).wait()
-        return carry
-
-    lax.fori_loop(1, devs, wait_c, 0)
-    rows = total_grad.shape[1]
-    cache_len = rows * devs
-    head_k = cbuf[:, :rows, :].reshape(cache_len, 128)
-    head_v = cbuf[:, rows:, :].reshape(cache_len, 128)
-    grad_prob = lax.dot_general(
-        head_v, grad, (((1,), (1,)), ((), ())), preferred_element_type=f32
-    )
-
+    o_cp[2].wait_recv()
+
+    @pl.when(inner)
+    def _():
+        relay(obuf, o_s, o_r).start()
+
+    wof_cp = {}
+    for k in range(1, PLANE):
+        for h in range(pair):
+            wo_cp[k, h].wait_recv()
+            wof_cp[k, h] = remote(
+                wobuf.at[k, mine + h],
+                wobuf.at[k, mine + h],
+                wof_s.at[k, h],
+                wof_r.at[k, h],
+                m,
+                1 - c,
+            )
+            wof_cp[k, h].start()
     qkv = cpart[0]
     for k in range(1, PLANE):
         rc_cp[k].wait_recv()
@@ -599,6 +546,17 @@
     own_kv = pltpu.make_async_copy(kv_part(m), kvr.at[m], loc.at[2])
     own_kv.start()
 
+    own_c.wait()
+
+    def wait_c(k, carry):
+        c_copy(k).wait()
+        return carry
+
+    lax.fori_loop(1, devs, wait_c, 0)
+    rows = total_grad.shape[1]
+    cache_len = rows * devs
+    head_k = cbuf[:, :rows, :].reshape(cache_len, 128)
+    head_v = cbuf[:, rows:, :].reshape(cache_len, 128)
     scale = 128 ** (-0.5)
     q_raw = qkv[:, :128]
     turned = jnp.concatenate([q_raw[:, 64:], q_raw[:, :64]], axis=1)
@@ -641,6 +599,48 @@
     prob = e_cache * inverse
     weight = prob.astype(bf16)
     weight_self = (e_self * inverse).astype(bf16)
+    for k in range(1, PLANE):
+        for h in range(pair):
+            wof_cp[k, h].wait_recv()
+
+    for kz in range(LINE):
+        if kz == 0:
+            block = og[...]
+        else:
+            if kz != 2:
+                o_cp[kz].wait_recv()
+            block = obuf[kz]
+        zz = (line + LINE - kz) % LINE
+
+        def add_d(k, carry):
+            term = lax.dot_general(
+                block, wobuf[k, zz], (((1,), (1,)), ((), ())), preferred_element_type=f32
+            )
+            if kz == 0:
+                dpart[k] = term
+            else:
+                dpart[k] = dpart[k] + term
+            return carry
+
+        lax.fori_loop(0, PLANE, add_d, 0)
+
+    rd_cp = {}
+    for k in range(1, PLANE):
+        rd_cp[k] = remote(dpart.at[k], drecv.at[k], rd_s.at[k], rd_r.at[k], back_chip(k), c)
+        rd_cp[k].start()
+
+    grad = dpart[0]
+    for k in range(1, PLANE):
+        rd_cp[k].wait_recv()
+        grad = grad + drecv[k]
+    grad = grad.astype(bf16)
+    grad_t = lax.dot_general(
+        eye, grad, (((1,), (1,)), ((), ())), preferred_element_type=f32
+    )
+    grad_prob = lax.dot_general(
+        head_v, grad, (((1,), (1,)), ((), ())), preferred_element_type=f32
+    )
+
     attended = lax.dot_general(
         head_v, weight, (((0,), (0,)), ((), ())), preferred_element_type=f32
     ) + jnp.dot(value_t, weight_self, preferred_element_type=f32)

time: 115 us -> 113 us (0.983)
  Pallas kernels: 104 us -> 101 us
    pallas_call x1, Pallas kernels: 104 us -> 101 us  [fused_device(): pl.pallas_call(fused_kernel, out_shape=jax.ShapeDtypeStruct(first_moment....]
where the time goes in v4:
time: 113 us; the launch traced here: 112 us
  Pallas kernels  101 us (89%)
  other arithmetic  8.67 us (8%)
  local copies, waits for them, and re-layouts  1.58 us (1%)
    pallas_call x1, Pallas kernels, fused_device(): pl.pallas_call(fused_kernel, out_shape=jax.ShapeDtypeStruct(first_moment....  101 us

profile of v4, /device:TPU:13, one launch (start us, length us, event | category | flops | bytes accessed | tf_op | source)
XLA Modules:
  0.0 112.2 jit_solution(17094076784617174549)
XLA Ops:
  0.6 1.7 %pad_maximum_fusion = bf16[8,2,8,8192]{3,2,0,1:T(8,128)(2,1)S(1)} fusion(bf16[8,1,8,8192]{3,2,0,1:T(8,128)(2,1)} %bitcast.57, bf16[8,1,8,8192]{3,2,0,1:T(8,128)(2,1)} %bitcast.58), kind=kLoop, calls=%fused_computation | loop fusion | flops 1048576 | bytes 4194304 | tf_op jit(solution)/shard_map/stack | solution.py:724
  2.4 0.0 copy-start.2
  2.4 0.0 copy-start.3
  2.4 0.0 copy-start.4
  2.4 0.0 copy-start.5
  2.4 1.5 %copy.20 = bf16[8,2,8,8192]{3,2,1,0:T(8,128)(2,1)} copy(bf16[8,2,8,8192]{3,2,0,1:T(8,128)(2,1)S(1)} %pad_maximum_fusion) | data formatting | bytes 4194304 | tf_op jit(solution)/shard_map/stack | solution.py:724
  3.9 0.0 copy-done.2
  4.0 0.0 copy-done.3
  4.0 0.7 pad_maximum_fusion.5
  4.7 0.0 copy-done.4
  4.7 0.2 reduce-window.4
  4.9 0.1 convert_reduce_fusion
  5.0 0.0 copy-done.5
  5.0 0.1 select_reduce_fusion.1
  5.1 0.6 fusion.18
  5.8 0.9 pad_maximum_fusion.3
  6.6 0.0 copy-start
  6.7 101.2 %shard_map.156 = f32[2,32,1024]{2,1,0:T(8,128)} custom-call(bf16[320,512]{1,0:T(8,128)(2,1)} %hid.1, bf16[320,512]{1,0:T(8,128)(2,1)} %og.1, f32[16,1,512]{2,1,0:T(1,128)} %bitcast.62, bf16[4,4,512,128]{3,2,1,0:T(8,128)(2,1)} %bitcast.56, bf16[128,8192]{1,0:T(8,128)(2,1)} %bitcast.55, bf16[128,8192]{1,0:T(8,128)(2,1)} %wout.1, bf16[8,64,128]{2,1,0:T(8,128)(2,1)} %bitcast.59, ...), custom_call_target="tpu_custom_call" | custom-call | tf_op jit(solution)/shard_map/pallas_call | solution.py:739
  107.8 0.0 copy-done
  107.9 0.0 copy-done.1
  107.9 1.8 %fusion.11 = (f32[32,1024]{1,0:T(8,128)}, f32[32,1024]{1,0:T(8,128)}) fusion(f32[32,1024]{1,0:T(8,128)S(1)} %copy-done.2, f32[2,32,1024]{2,1,0:T(8,128)S(1)} %copy-done, f32[2,32,1024]{2,1,0:T(8,128)S(1)} %copy-done.1, f32[2,32,1024]{2,1,0:T(8,128)} %shard_map.156, f32[32,1024]{1,0:T(8,128)S(1)} %copy-done.3), kind=kLoop, calls=%fused_computation.22 | loop fusion | flops 786432 | bytes 1310720 | tf_op jit(solution)/shard_map/sub | solution.py:89
  109.7 1.0 fusion.12
  110.8 0.7 pad_maximum_fusion.1
  111.5 0.7 pad_maximum_fusion.2
  (10 shorter events, 0.1 us)
Async XLA Ops:
  2.4 1.5 %copy-start.2 = (f32[32,1024]{1,0:T(8,128)S(1)}, f32[32,1024]{1,0:T(8,128)}, u32[]{:S(2)}) copy-start(f32[32,1024]{1,0:T(8,128)} %param.21) | copy-start | bytes 393220
  2.4 1.6 %copy-start.3 = (f32[32,1024]{1,0:T(8,128)S(1)}, f32[32,1024]{1,0:T(8,128)}, u32[]{:S(2)}) copy-start(f32[32,1024]{1,0:T(8,128)} %param.20) | copy-start | bytes 393220
  2.4 2.3 %copy-start.4 = (s32[1,4]{1,0:T(1,128)S(1)}, s32[1,4]{1,0:T(1,128)}, u32[]{:S(2)}) copy-start(s32[1,4]{1,0:T(1,128)} %lengths.1) | copy-start | bytes 52
  2.4 2.6 %copy-start.5 = (s32[1,4]{1,0:T(1,128)S(1)}, s32[1,4]{1,0:T(1,128)}, u32[]{:S(2)}) copy-start(s32[1,4]{1,0:T(1,128)} %param.25) | copy-start | bytes 52
  6.6 101.2 %copy-start = (f32[2,32,1024]{2,1,0:T(8,128)S(1)}, f32[2,32,1024]{2,1,0:T(8,128)}, u32[]{:S(2)}) copy-start(f32[2,32,1024]{2,1,0:T(8,128)} %param.22) | copy-start | bytes 786436
  6.7 101.2 %copy-start.1 = (f32[2,32,1024]{2,1,0:T(8,128)S(1)}, f32[2,32,1024]{2,1,0:T(8,128)}, u32[]{:S(2)}) copy-start(f32[2,32,1024]{2,1,0:T(8,128)} %param.23) | copy-start | bytes 786436

commit v5 on v4

--- a/solution.py
+++ b/solution.py
@@ -411,11 +411,6 @@
 
     lax.fori_loop(1, devs, start_c, 0)
 
-    for k in (2, 1, 3):
-        o_cp[k] = remote(og, obuf.at[k], o_s.at[k], o_r.at[k], line_chip(k), c)
-        when(direct(k), o_cp[k].start)
-
-    send_rows(wout, wobuf, wo_s, wo_r, wo_cp)
     h_cp[2].wait_recv()
 
     @pl.when(inner)
@@ -434,6 +429,11 @@
             wkf_cp[k, h] = remote(part, part, wkf_s.at[k, h], wkf_r.at[k, h], m, 1 - c)
             wkf_cp[k, h].start()
 
+    for k in (2, 1, 3):
+        o_cp[k] = remote(og, obuf.at[k], o_s.at[k], o_r.at[k], line_chip(k), c)
+        when(direct(k), o_cp[k].start)
+
+    send_rows(wout, wobuf, wo_s, wo_r, wo_cp)
     unit = (
         lax.broadcasted_iota(jnp.int32, (128, 128), 0)
         == lax.broadcasted_iota(jnp.int32, (128, 128), 1)

time: 113 us -> 112 us (level)
  no operation moved by 1% of the time
where the time goes in v5:
time: 112 us
  Pallas kernels  101 us (90%)
  other arithmetic  8.67 us (8%)
  local copies, waits for them, and re-layouts  1.58 us (1%)
    pallas_call x1, Pallas kernels, fused_device(): pl.pallas_call(fused_kernel, out_shape=jax.ShapeDtypeStruct(first_moment....  101 us

profile of v5, /device:TPU:13, one launch (start us, length us, event | category | flops | bytes accessed | tf_op | source)
XLA Modules:
  0.0 112.2 jit_solution(13307658893846664773)
XLA Ops:
  0.6 1.7 %pad_maximum_fusion = bf16[8,2,8,8192]{3,2,0,1:T(8,128)(2,1)S(1)} fusion(bf16[8,1,8,8192]{3,2,0,1:T(8,128)(2,1)} %bitcast.57, bf16[8,1,8,8192]{3,2,0,1:T(8,128)(2,1)} %bitcast.58), kind=kLoop, calls=%fused_computation | loop fusion | flops 1048576 | bytes 4194304 | tf_op jit(solution)/shard_map/stack | solution.py:724
  2.4 0.0 copy-start.2
  2.4 0.0 copy-start.3
  2.4 0.0 copy-start.4
  2.4 0.0 copy-start.5
  2.4 1.5 %copy.20 = bf16[8,2,8,8192]{3,2,1,0:T(8,128)(2,1)} copy(bf16[8,2,8,8192]{3,2,0,1:T(8,128)(2,1)S(1)} %pad_maximum_fusion) | data formatting | bytes 4194304 | tf_op jit(solution)/shard_map/stack | solution.py:724
  3.9 0.0 copy-done.2
  4.0 0.0 copy-done.3
  4.0 0.7 pad_maximum_fusion.5
  4.7 0.0 copy-done.4
  4.7 0.2 reduce-window.4
  4.9 0.1 convert_reduce_fusion
  5.0 0.0 copy-done.5
  5.0 0.1 select_reduce_fusion.1
  5.1 0.6 fusion.18
  5.8 0.9 pad_maximum_fusion.3
  6.6 0.0 copy-start
  6.7 101.2 %shard_map.156 = f32[2,32,1024]{2,1,0:T(8,128)} custom-call(bf16[320,512]{1,0:T(8,128)(2,1)} %hid.1, bf16[320,512]{1,0:T(8,128)(2,1)} %og.1, f32[16,1,512]{2,1,0:T(1,128)} %bitcast.62, bf16[4,4,512,128]{3,2,1,0:T(8,128)(2,1)} %bitcast.56, bf16[128,8192]{1,0:T(8,128)(2,1)} %bitcast.55, bf16[128,8192]{1,0:T(8,128)(2,1)} %wout.1, bf16[8,64,128]{2,1,0:T(8,128)(2,1)} %bitcast.59, ...), custom_call_target="tpu_custom_call" | custom-call | tf_op jit(solution)/shard_map/pallas_call | solution.py:739
  107.8 0.0 copy-done
  107.8 0.0 copy-done.1
  107.8 1.8 %fusion.11 = (f32[32,1024]{1,0:T(8,128)}, f32[32,1024]{1,0:T(8,128)}) fusion(f32[32,1024]{1,0:T(8,128)S(1)} %copy-done.2, f32[2,32,1024]{2,1,0:T(8,128)S(1)} %copy-done, f32[2,32,1024]{2,1,0:T(8,128)S(1)} %copy-done.1, f32[2,32,1024]{2,1,0:T(8,128)} %shard_map.156, f32[32,1024]{1,0:T(8,128)S(1)} %copy-done.3), kind=kLoop, calls=%fused_computation.22 | loop fusion | flops 786432 | bytes 1310720 | tf_op jit(solution)/shard_map/sub | solution.py:89
  109.7 1.0 fusion.12
  110.7 0.7 pad_maximum_fusion.1
  111.5 0.7 pad_maximum_fusion.2
  (10 shorter events, 0.1 us)
Async XLA Ops:
  2.4 1.5 %copy-start.2 = (f32[32,1024]{1,0:T(8,128)S(1)}, f32[32,1024]{1,0:T(8,128)}, u32[]{:S(2)}) copy-start(f32[32,1024]{1,0:T(8,128)} %param.21) | copy-start | bytes 393220
  2.4 1.6 %copy-start.3 = (f32[32,1024]{1,0:T(8,128)S(1)}, f32[32,1024]{1,0:T(8,128)}, u32[]{:S(2)}) copy-start(f32[32,1024]{1,0:T(8,128)} %param.20) | copy-start | bytes 393220
  2.4 2.3 %copy-start.4 = (s32[1,4]{1,0:T(1,128)S(1)}, s32[1,4]{1,0:T(1,128)}, u32[]{:S(2)}) copy-start(s32[1,4]{1,0:T(1,128)} %lengths.1) | copy-start | bytes 52
  2.4 2.6 %copy-start.5 = (s32[1,4]{1,0:T(1,128)S(1)}, s32[1,4]{1,0:T(1,128)}, u32[]{:S(2)}) copy-start(s32[1,4]{1,0:T(1,128)} %param.25) | copy-start | bytes 52
  6.6 101.2 %copy-start = (f32[2,32,1024]{2,1,0:T(8,128)S(1)}, f32[2,32,1024]{2,1,0:T(8,128)}, u32[]{:S(2)}) copy-start(f32[2,32,1024]{2,1,0:T(8,128)} %param.22) | copy-start | bytes 786436
  6.7 101.2 %copy-start.1 = (f32[2,32,1024]{2,1,0:T(8,128)S(1)}, f32[2,32,1024]{2,1,0:T(8,128)}, u32[]{:S(2)}) copy-start(f32[2,32,1024]{2,1,0:T(8,128)} %param.23) | copy-start | bytes 786436
